TPU v7x, 32 devices: a whole 2x2x4 slice. The times are simulated.
32 devices in a mesh: batch: 8 (over z, x), rows: 4 (over y, core).
Axes of the slice: x: 2, y: 2, z: 4, core: 2. Of those that a mesh axis runs over, the one named last changes fastest.
Arguments:
- inputs: bfloat16 [384, 16, 16, 891], P('batch', 'rows'), may hold values from -14 to 14
- small_flags: int32 [384], P('batch'), may hold values 0 or 1
- norm_params: float32 [2, 1947], replicated, may hold values from -1 to 2.1
- norm_moment: float32 [2, 1947], replicated, may hold values from -384 to 384
- w_bottleneck: float32 [891, 132], replicated, may hold values from -0.1875 to 0.1875
- w_growth: float32 [1188, 33], replicated, may hold values from -0.1875 to 0.1875
- w_transition: float32 [924, 462], replicated, may hold values from -0.1875 to 0.1875
- m_bottleneck: float32 [891, 132], replicated, may hold values from -896 to 896
- m_growth: float32 [1188, 33], replicated, may hold values from -896 to 896
- m_transition: float32 [924, 462], replicated, may hold values from -896 to 896
- cotangent: bfloat16 [384, 8, 8, 462], P(('batch', 'rows')), may hold values from -7 to 7
Outputs:
- pooled: bfloat16 [384, 8, 8, 462], P(('batch', 'rows'))
- input_grad: bfloat16 [384, 16, 16, 891], P('batch', 'rows')
- norm_moment_new: float32 [2, 1947], replicated
- norm_params_new: float32 [2, 1947], replicated
- m_bottleneck_new: float32 [891, 132], replicated
- m_growth_new: float32 [1188, 33], replicated
- m_transition_new: float32 [924, 462], replicated
- w_bottleneck_new: float32 [891, 132], replicated
- w_growth_new: float32 [1188, 33], replicated
- w_transition_new: float32 [924, 462], replicated
All inputs are finite; a program needn't handle non-finite values. No bound on the sum of `small_flags` on one device may be relied on, other than what follows from the above.
Results may differ from a plain program's by a relative error of at most 0.0089.
Values may be sent and summed in bfloat16 or wider, within the bound.
A program may use at most 192 MiB of HBM per device.

v0:
```python
import jax
import jax.numpy as jnp
from jax import lax
from jax.sharding import PartitionSpec as P

SMALL = 12
NS_STEPS = 5


EPSILON = 1e-05
MOMENTUM_DECAY = 0.9
MUON_RATE = 0.5
NORM_RATE = 1.0
QUINTIC_A = 3.4445
QUINTIC_B = -4.775
QUINTIC_C = 2.0315
TINY = 1e-07
PRECISE = lax.Precision.HIGHEST


def with_halo(value, sides, width):
    for axis, dim in sides:
        count, length = (lax.axis_size(axis), value.shape[dim])
        up = [(i, (i + 1) % count) for i in range(count - 1)]
        down = [(j, i) for i, j in up]
        last = lax.slice_in_dim(value, length - width, length, axis=dim)
        first = lax.slice_in_dim(value, 0, width, axis=dim)
        before = lax.ppermute(last, axis, up)
        after = lax.ppermute(first, axis, down)
        value = jnp.concatenate([before, value, after], axis=dim)
    return value


def band_mask(small_flags, row_index, band_rows, map_width):
    row_ids = row_index * band_rows + lax.broadcasted_iota(jnp.int32, (band_rows, map_width), 0)
    col_ids = lax.broadcasted_iota(jnp.int32, (band_rows, map_width), 1)
    inside = jnp.where((row_ids < SMALL) & (col_ids < SMALL), 1.0, 0.0).astype(jnp.float32)
    is_small = (small_flags > 0)[:, None, None]
    return jnp.where(is_small, inside[None], jnp.ones_like(inside)[None])


def forward_taps(rimmed):
    images_here, rim_height, map_width, channels = rimmed.shape
    band_rows = rim_height - 2
    padded = jnp.pad(rimmed, ((0, 0), (0, 0), (1, 1), (0, 0)))
    pieces = [
        padded[:, tap_row : tap_row + band_rows, tap_col : tap_col + map_width, :]
        for tap_row in range(3)
        for tap_col in range(3)
    ]
    return jnp.stack(pieces, axis=-1).reshape(images_here, band_rows, map_width, channels * 9)


def backward_taps(rimmed):
    images_here, rim_height, map_width, channels = rimmed.shape
    band_rows = rim_height - 2
    padded = jnp.pad(rimmed, ((0, 0), (0, 0), (1, 1), (0, 0)))
    pieces = [
        padded[:, 2 - tap_row : 2 - tap_row + band_rows, 2 - tap_col : 2 - tap_col + map_width, :]
        for tap_row in range(3)
        for tap_col in range(3)
    ]
    return jnp.stack(pieces, axis=-2).reshape(images_here, band_rows, map_width, 9 * channels)


def silu_slope(values):
    sigma = jax.nn.sigmoid(values)
    return sigma * (1.0 + values * (1.0 - sigma))


def masked_sums(values, cell_mask):
    weighted = values * cell_mask
    return (jnp.sum(weighted, axis=(0, 1, 2)), jnp.sum(weighted * values, axis=(0, 1, 2)))


def quintic(row_part, gram_part):
    poly_part = QUINTIC_B * gram_part + QUINTIC_C * jnp.dot(gram_part, gram_part, precision=PRECISE)
    return QUINTIC_A * row_part + jnp.dot(row_part, poly_part, precision=PRECISE)


def gram_of(row_part):
    return jnp.dot(row_part.T, row_part, precision=PRECISE)


def orthogonal(moment):
    current = moment / (jnp.sqrt(jnp.sum(moment * moment)) + TINY)
    for sweep_index in range(NS_STEPS):
        current = quintic(current, gram_of(current))
    return current


def per_device(
    inputs,
    small_flags,
    norm_params,
    norm_moment,
    w_bottleneck,
    w_growth,
    w_transition,
    m_bottleneck,
    m_growth,
    m_transition,
    cotangent,
):
    row_index = lax.axis_index("rows")
    images_here = inputs.shape[0]
    band_rows = inputs.shape[1]
    map_width = inputs.shape[2]
    in_chans = inputs.shape[3]
    mid_chans = w_bottleneck.shape[1]
    new_chans = w_growth.shape[1]
    valid_cells = band_mask(small_flags, row_index, band_rows, map_width)
    cell_mask = valid_cells[..., None]
    all_gains = norm_params[0]
    all_shifts = norm_params[1]
    gain_first = all_gains[:in_chans]
    shift_first = all_shifts[:in_chans]
    gain_middle = all_gains[in_chans : in_chans + mid_chans]
    shift_middle = all_shifts[in_chans : in_chans + mid_chans]
    gain_last = all_gains[in_chans + mid_chans :]
    shift_last = all_shifts[in_chans + mid_chans :]
    features = inputs.astype(jnp.float32)
    local_sum, local_square = masked_sums(features, cell_mask)
    first_sum, first_square, cell_count = lax.psum(
        (local_sum, local_square, jnp.sum(valid_cells)), ("batch", "rows")
    )
    first_mean = first_sum / cell_count
    first_scale = lax.rsqrt(first_square / cell_count - first_mean * first_mean + EPSILON)
    first_hat = (features - first_mean) * first_scale
    first_pre = first_hat * gain_first + shift_first
    first_act = (jax.nn.silu(first_pre) * cell_mask).astype(jnp.bfloat16)
    w_first = w_bottleneck.astype(jnp.bfloat16)
    bottleneck = jnp.dot(first_act, w_first, preferred_element_type=jnp.float32)
    local_sum, local_square = masked_sums(bottleneck, cell_mask)
    middle_sum, middle_square = lax.psum((local_sum, local_square), ("batch", "rows"))
    middle_mean = middle_sum / cell_count
    middle_scale = lax.rsqrt(middle_square / cell_count - middle_mean * middle_mean + EPSILON)
    middle_hat = (bottleneck - middle_mean) * middle_scale
    middle_pre = middle_hat * gain_middle + shift_middle
    middle_act = (jax.nn.silu(middle_pre) * cell_mask).astype(jnp.bfloat16)
    rimmed = with_halo(middle_act, (("rows", 1),), 1)
    patches = forward_taps(rimmed)
    w_taps = w_growth.astype(jnp.bfloat16)
    growth = jnp.dot(patches, w_taps, preferred_element_type=jnp.float32)
    local_sum, local_square = masked_sums(growth, cell_mask)
    growth_sum, growth_square = lax.psum((local_sum, local_square), ("batch", "rows"))
    growth_mean = growth_sum / cell_count
    growth_scale = lax.rsqrt(growth_square / cell_count - growth_mean * growth_mean + EPSILON)
    growth_hat = (growth - growth_mean) * growth_scale
    concat_hat = jnp.concatenate([first_hat, growth_hat], axis=-1)
    concat_scale = jnp.concatenate([first_scale, growth_scale])
    transition_in = ((concat_hat * gain_last + shift_last) * cell_mask).astype(jnp.bfloat16)
    w_last = w_transition.astype(jnp.bfloat16)
    transition = jnp.dot(transition_in, w_last, preferred_element_type=jnp.float32)
    trans_chans = transition.shape[-1]
    grouped = transition.reshape(images_here, band_rows // 2, 2, map_width // 2, 2, trans_chans)
    pooled = (0.25 * jnp.sum(grouped, axis=(2, 4))).astype(jnp.bfloat16)
    pooled_out = lax.all_to_all(pooled, "rows", split_axis=0, concat_axis=1, tiled=True)
    returned = lax.all_to_all(cotangent, "rows", split_axis=1, concat_axis=0, tiled=True)
    grad_trans = jnp.repeat(jnp.repeat(returned, 2, axis=1), 2, axis=2) * 0.25
    grad_w_last = jnp.einsum(
        "abcd,abce->de", transition_in, grad_trans, preferred_element_type=jnp.float32
    )
    grad_last_norm = (
        jnp.einsum("abce,de->abcd", grad_trans, w_last, preferred_element_type=jnp.float32)
        * cell_mask
    )
    last_gain_local = jnp.sum(grad_last_norm * concat_hat, axis=(0, 1, 2))
    last_shift_local = jnp.sum(grad_last_norm, axis=(0, 1, 2))
    last_gain_grad, last_shift_grad = lax.psum(
        (last_gain_local, last_shift_local), ("batch", "rows")
    )
    grad_joined = (
        cell_mask
        * gain_last
        * concat_scale
        * (grad_last_norm - (last_shift_grad + concat_hat * last_gain_grad) / cell_count)
    )
    grad_growth = grad_joined[..., in_chans:].astype(jnp.bfloat16)
    grad_w_taps = jnp.einsum(
        "abcd,abce->de", patches, grad_growth, preferred_element_type=jnp.float32
    )
    grad_rimmed = with_halo(grad_growth, (("rows", 1),), 1)
    w_flipped = (
        w_taps.reshape(mid_chans, 9, new_chans).transpose(1, 2, 0).reshape(9 * new_chans, mid_chans)
    )
    grad_middle_act = (
        jnp.dot(backward_taps(grad_rimmed), w_flipped, preferred_element_type=jnp.float32)
        * cell_mask
    )
    grad_middle = grad_middle_act * silu_slope(middle_pre)
    middle_gain_local = jnp.sum(grad_middle * middle_hat, axis=(0, 1, 2))
    middle_shift_local = jnp.sum(grad_middle, axis=(0, 1, 2))
    middle_gain_grad, middle_shift_grad = lax.psum(
        (middle_gain_local, middle_shift_local), ("batch", "rows")
    )
    grad_bottleneck = (
        cell_mask
        * gain_middle
        * middle_scale
        * (grad_middle - (middle_shift_grad + middle_hat * middle_gain_grad) / cell_count)
    ).astype(jnp.bfloat16)
    grad_w_first = jnp.einsum(
        "abcd,abce->de", first_act, grad_bottleneck, preferred_element_type=jnp.float32
    )
    grad_first_act = (
        jnp.einsum("abce,de->abcd", grad_bottleneck, w_first, preferred_element_type=jnp.float32)
        * cell_mask
    )
    grad_first = grad_first_act * silu_slope(first_pre)
    first_gain_local = jnp.sum(grad_first * first_hat, axis=(0, 1, 2))
    first_shift_local = jnp.sum(grad_first, axis=(0, 1, 2))
    first_gain_grad, first_shift_grad = lax.psum(
        (first_gain_local, first_shift_local), ("batch", "rows")
    )
    first_back = (
        cell_mask
        * gain_first
        * first_scale
        * (grad_first - (first_shift_grad + first_hat * first_gain_grad) / cell_count)
    )
    input_grad = (grad_joined[..., :in_chans] + first_back).astype(jnp.bfloat16)
    grad_w_first, grad_w_taps, grad_w_last = lax.psum(
        (grad_w_first, grad_w_taps, grad_w_last), ("batch", "rows")
    )
    gain_grads = jnp.concatenate([first_gain_grad, middle_gain_grad, last_gain_grad])
    shift_grads = jnp.concatenate([first_shift_grad, middle_shift_grad, last_shift_grad])
    norm_moment_new = MOMENTUM_DECAY * norm_moment + jnp.stack([gain_grads, shift_grads])
    norm_params_new = norm_params - NORM_RATE * norm_moment_new / jnp.sqrt(cell_count)
    new_moments = (
        MOMENTUM_DECAY * m_bottleneck + grad_w_first,
        MOMENTUM_DECAY * m_growth + grad_w_taps,
        MOMENTUM_DECAY * m_transition + grad_w_last,
    )
    old_weights = (w_bottleneck, w_growth, w_transition)
    new_weights = [
        weight - MUON_RATE * orthogonal(moment) for weight, moment in zip(old_weights, new_moments)
    ]
    return (
        pooled_out,
        input_grad,
        norm_moment_new,
        norm_params_new,
        new_moments[0],
        new_moments[1],
        new_moments[2],
        new_weights[0],
        new_weights[1],
        new_weights[2],
    )


def solution(mesh):
    return jax.shard_map(
        per_device,
        mesh=mesh,
        in_specs=(
            P("batch", "rows", None, None),
            P("batch"),
            P(),
            P(),
            P(),
            P(),
            P(),
            P(),
            P(),
            P(),
            P(("batch", "rows"), None, None, None),
        ),
        out_specs=(
            P(("batch", "rows"), None, None, None),
            P("batch", "rows", None, None),
            P(),
            P(),
            P(),
            P(),
            P(),
            P(),
            P(),
            P(),
        ),
        check_vma=False,
    )
```

profile of v0, /device:TPU:0, one launch (start us, length us, event | category | flops | bytes accessed | tf_op | source)
XLA Modules:
  0.0 729.4 jit_solution(10403478373970960991)
XLA Ops:
  14.8 42.3 %all-reduce.7 = (f32[891]{0:T(1024)S(1)}, f32[]{:T(128)}, f32[891]{0:T(1024)S(1)}) all-reduce(f32[891]{0:T(1024)S(1)} %get-tuple-element.15, f32[]{:T(128)} %get-tuple-element.68, f32[891]{0:T(1024)S(1)} %get-tuple-element.14), channel_id=1, replica_groups=mesh['batch'=8,'rows'=4] {'batch','rows'}, use_global_device_ids=true, to_apply=%region_5.6 | all-reduce | flops 1783 | bytes 14264 | tf_op jit(solution)/shard_map/psum | solution.py:124
  57.7 9.1 %fusion.3 = (f32[48,4,16,891]{3,2,1,0:T(8,128)}, bf16[48,4,16,891]{3,2,1,0:T(8,128)(2,1)S(1)}) fusion(bf16[48,4,16,891]{3,2,1,0:T(8,128)(2,1)} %param.11, f32[891]{0:T(1024)S(1)} %get-tuple-element.67, f32[891]{0:T(1024)S(1)} %get-tuple-element.66, f32[48,4,16]{2,1,0:T(4,128)S(1)} %get-tuple-element.69, f32[891]{0:T(1024)S(1)} %get-tuple-element.23, ...), kind=kLoop, calls=%fused_computation.11 | loop fusion | flops 30108672 | bytes 21923760 | tf_op jit(solution)/shard_map/mul | solution.py:129
  69.2 40.3 %all-reduce.6 = (f32[132]{0:T(256)S(1)}, f32[132]{0:T(256)S(1)}) all-reduce(f32[132]{0:T(256)S(1)} %get-tuple-element.17, f32[132]{0:T(256)S(1)} %get-tuple-element.16), channel_id=1, replica_groups=mesh['batch'=8,'rows'=4] {'batch','rows'}, use_global_device_ids=true, to_apply=%region_7.8 | all-reduce | flops 264 | bytes 2112 | tf_op jit(solution)/shard_map/psum | solution.py:135
  118.3 6.3 all-to-all-start.1
  149.5 30.6 %copy.56 = bf16[48,4,16,132,9]{0,2,4,3,1:T(8,128)(2,1)} copy(bf16[48,4,16,132,9]{3,2,1,0,4:T(8,128)(2,1)} %fusion.37) | data formatting | bytes 14598144 | tf_op jit(solution)/shard_map/stack | solution.py:51
  180.1 28.9 %copy.57 = bf16[48,4,16,1188]{3,2,1,0:T(8,128)(2,1)} copy(bf16[48,4,16,1188]{0,2,3,1:T(8,128)(2,1)} %bitcast.220) | data formatting | bytes 14598144 | tf_op jit(solution)/shard_map/reshape | solution.py:51
  209.0 6.6 fusion.36
  215.5 40.7 %all-reduce.5 = (f32[33]{0:T(128)S(1)}, f32[33]{0:T(128)S(1)}) all-reduce(f32[33]{0:T(128)S(1)} %get-tuple-element.21, f32[33]{0:T(128)S(1)} %get-tuple-element.20), channel_id=1, replica_groups=mesh['batch'=8,'rows'=4] {'batch','rows'}, use_global_device_ids=true, to_apply=%region_11.12 | all-reduce | flops 66 | bytes 528 | tf_op jit(solution)/shard_map/psum | solution.py:146
  264.4 12.8 %multiply_reduce_fusion.1 = (f32[924]{0:T(1024)S(1)}, f32[924]{0:T(1024)S(1)}, f32[48,4,16,924]{3,2,1,0:T(8,128)}) fusion(f32[48,4,16]{2,1,0:T(4,128)S(1)} %get-tuple-element.69, f32[48,4,16,33]{3,2,1,0:T(8,128)S(1)} %copy-done.4, f32[48,4,16,891]{3,2,1,0:T(8,128)} %get-tuple-element.58, f32[924,462]{1,0:T(8,128)S(1)} %copy-done.9, ...), kind=kOutput, calls=%fused_computation.10 | convolution fusion | flops 2637417472 | bytes 27273984 | tf_op jit(solution)/shard_map/abce,de->abcd/dot_general | solution.py:165
  277.1 40.1 %all-reduce.4 = (f32[924]{0:T(1024)S(1)}, f32[924]{0:T(1024)S(1)}) all-reduce(f32[924]{0:T(1024)S(1)} %get-tuple-element.11, f32[924]{0:T(1024)S(1)} %get-tuple-element.10), channel_id=1, replica_groups=mesh['batch'=8,'rows'=4] {'batch','rows'}, use_global_device_ids=true, to_apply=%region_18.19 | all-reduce | flops 1848 | bytes 14784 | tf_op jit(solution)/shard_map/psum | solution.py:170
  317.3 17.4 %fusion.101 = (bf16[48,4,16,924]{3,2,1,0:T(8,128)(2,1)S(1)}, f32[48,4,16,924]{3,2,1,0:T(8,128)}, bf16[48,4,16,924]{3,2,1,0:T(8,128)(2,1)S(1)}) fusion(f32[]{:T(128)} %get-tuple-element.35, f32[924]{0:T(1024)S(1)} %get-tuple-element.28, f32[48,4,16,33]{3,2,1,0:T(8,128)} %subtract_multiply_fusion.2, f32[48,4,16,891]{3,2,1,0:T(8,128)} %get-tuple-element.58, ...), kind=kLoop, calls=%fused_computation.199 | loop fusion | flops 39739392 | bytes 45447220 | tf_op jit(solution)/shard_map/convert
  337.7 6.9 fusion.33
  344.6 5.6 fusion.71
  350.2 12.8 %fusion.25 = f32[1188,33]{0,1:T(8,128)} fusion(bf16[48,4,16,1188]{0,2,3,1:T(8,128)(2,1)} %bitcast.221, bf16[48,4,16,33]{3,2,1,0:T(8,128)(2,1)} %slice.151), kind=kOutput, calls=%fused_computation.57 | convolution fusion | flops 240869376 | bytes 7658640 | tf_op jit(solution)/shard_map/abcd,abce->de/dot_general | solution.py:180
  365.5 8.4 %reshape.97 = f32[48,2,2,8,2,462]{5,4,3,2,1,0:T(2,128)} reshape(f32[48,4,16,462]{3,2,1,0:T(8,128)} %fusion.71) | data formatting | bytes 11354112 | tf_op jit(solution)/shard_map/reshape | solution.py:156
  373.9 9.2 %reduce_sum.160 = f32[48,2,8,462]{3,2,1,0:T(8,128)} reduce(f32[48,2,2,8,2,462]{5,4,3,2,1,0:T(2,128)} %reshape.97, f32[]{:T(128)} %constant.21.clone.1), dimensions={2,4}, to_apply=%region_14.15 | reduce | flops 1064448 | bytes 7096324 | tf_op jit(solution)/shard_map/reduce_sum | solution.py:157
  385.7 6.5 all-to-all-start
  408.1 40.8 %all-reduce.3 = (f32[132]{0:T(256)S(1)}, f32[132]{0:T(256)S(1)}) all-reduce(f32[132]{0:T(256)S(1)} %get-tuple-element.19, f32[132]{0:T(256)S(1)} %get-tuple-element.18), channel_id=1, replica_groups=mesh['batch'=8,'rows'=4] {'batch','rows'}, use_global_device_ids=true, to_apply=%region_22.23 | all-reduce | flops 264 | bytes 2112 | tf_op jit(solution)/shard_map/psum | solution.py:194
  453.2 10.1 %fusion.53 = f32[891,132]{0,1:T(8,128)} fusion(bf16[48,4,16,132]{3,2,1,0:T(8,128)(2,1)S(1)} %multiply_convert_fusion.2, bf16[48,4,16,891]{3,2,1,0:T(8,128)(2,1)} %copy-done.5), kind=kOutput, calls=%fused_computation.106 | convolution fusion | flops 722608128 | bytes 6755760 | tf_op jit(solution)/shard_map/abcd,abce->de/dot_general | solution.py:203
  463.3 11.4 %fusion.98 = (f32[891]{0:T(1024)S(1)}, f32[891]{0:T(1024)S(1)}, f32[48,4,16,891]{3,2,1,0:T(8,128)}) fusion(f32[891]{0:T(1024)S(1)} %get-tuple-element.67, f32[891]{0:T(1024)S(1)} %copy-done.31, bf16[48,4,16,891]{3,2,1,0:T(8,128)(2,1)} %param.11, f32[891]{0:T(1024)S(1)} %copy-done.39, f32[891]{0:T(1024)S(1)} %copy-done.29, ...), kind=kOutput, calls=%fused_computation.197 | convolution fusion | flops 769255552 | bytes 17738040 | tf_op jit(solution)/shard_map/abce,de->abcd/dot_general | solution.py:207
  474.7 40.1 %all-reduce.2 = (f32[891]{0:T(1024)S(1)}, f32[891]{0:T(1024)S(1)}) all-reduce(f32[891]{0:T(1024)S(1)} %get-tuple-element.13, f32[891]{0:T(1024)S(1)} %get-tuple-element.12), channel_id=1, replica_groups=mesh['batch'=8,'rows'=4] {'batch','rows'}, use_global_device_ids=true, to_apply=%region_26.27 | all-reduce | flops 1782 | bytes 14256 | tf_op jit(solution)/shard_map/psum | solution.py:213
  514.8 14.2 %fusion.5 = bf16[48,4,16,891]{3,2,1,0:T(8,128)(2,1)} fusion(f32[48,4,16,924]{3,2,1,0:T(8,128)} %get-tuple-element.50, f32[48,4,16,891]{3,2,1,0:T(8,128)} %get-tuple-element.73, bf16[48,4,16,891]{3,2,1,0:T(8,128)(2,1)} %param.11, f32[]{:T(128)} %get-tuple-element.35, f32[891]{0:T(1024)S(1)} %get-tuple-element.24, f32[891]{0:T(1024)S(1)} %get-tuple-element.25, ...), kind=kLoop, calls=%fused_computation.14 | loop fusion | flops 32845824 | bytes 32875936 | tf_op jit(solution)/shard_map/convert_element_type | solution.py:222
  531.9 120.9 %all-reduce.11.cloned.1.call-done = (f32[891,132]{0,1:T(8,128)}, f32[1188,33]{0,1:T(8,128)}, f32[924,462]{1,0:T(8,128)}) async-done(((f32[891,132]{0,1:T(8,128)}, f32[1188,33]{0,1:T(8,128)}, f32[924,462]{1,0:T(8,128)}), (f32[891,132]{0,1:T(8,128)}, f32[1188,33]{0,1:T(8,128)}, f32[924,462]{1,0:T(8,128)})) %all-reduce.11.cloned.1.call-update) | async-done | bytes 2334832 | tf_op jit(solution)/shard_map/psum | solution.py:223
  657.3 6.0 fusion.84
  (201 shorter events, 143.6 us)
Async XLA Ops:
  8.0 58.8 %copy-start.28 = (f32[891]{0:T(1024)}, f32[891]{0:T(1024)S(1)}, u32[]{:S(2)}) copy-start(f32[891]{0:T(1024)S(1)} %get-tuple-element.22) | copy-start | bytes 10696
  8.0 58.8 %copy-start.38 = (f32[891]{0:T(1024)}, f32[891]{0:T(1024)S(1)}, u32[]{:S(2)}) copy-start(f32[891]{0:T(1024)S(1)} %get-tuple-element.23) | copy-start | bytes 10696
  8.8 101.4 %copy-start.32 = (f32[1,132]{1,0:T(1,128)}, f32[1,132]{1,0:T(1,128)S(1)}, u32[]{:S(2)}) copy-start(f32[1,132]{1,0:T(1,128)S(1)} %get-tuple-element.64) | copy-start | bytes 1588
  8.8 101.4 %copy-start.41 = (f32[1,132]{1,0:T(1,128)}, f32[1,132]{1,0:T(1,128)S(1)}, u32[]{:S(2)}) copy-start(f32[1,132]{1,0:T(1,128)S(1)} %get-tuple-element.65) | copy-start | bytes 1588
  57.7 9.1 %copy-start.19 = (f32[891,132]{0,1:T(8,128)S(1)}, f32[891,132]{0,1:T(8,128)}, u32[]{:S(2)}) copy-start(f32[891,132]{0,1:T(8,128)} %param.15) | copy-start | bytes 1411348
  113.1 12.1 %copy-start.15 = (f32[1188,33]{0,1:T(8,128)S(1)}, f32[1188,33]{0,1:T(8,128)}, u32[]{:S(2)}) copy-start(f32[1188,33]{0,1:T(8,128)} %param.16) | copy-start | bytes 470452
  114.0 14.8 %collective-permute-start = (bf16[48,1,16,132]{3,2,1,0:T(8,128)(2,1)}, bf16[48,1,16,132]{3,2,1,0:T(8,128)(2,1)}, u32[]{:S(2)}, u32[]{:S(2)}) collective-permute-start(bf16[48,1,16,132]{3,2,1,0:T(8,128)(2,1)} %get-tuple-element.60), channel_id=1, source_target_pairs={{0,1},{1,2},{2,3},{4,5},{5,6},{6,7},{8,9},{9,10},{10,11},{12,13},{... | collective-permute-start | bytes 608264 | tf_op jit(solution)/shard_map/ppermute | solution.py:28
  116.0 12.8 %collective-permute-start.1 = (bf16[48,1,16,132]{3,2,1,0:T(8,128)(2,1)}, bf16[48,1,16,132]{3,2,1,0:T(8,128)(2,1)}, u32[]{:S(2)}, u32[]{:S(2)}) collective-permute-start(bf16[48,1,16,132]{3,2,1,0:T(8,128)(2,1)} %get-tuple-element.61), channel_id=1, source_target_pairs={{1,0},{2,1},{3,2},{5,4},{6,5},{7,6},{9,8},{10,9},{11,10},{13,12},{... | collective-permute-start | bytes 608264 | tf_op jit(solution)/shard_map/ppermute | solution.py:29
  118.3 141.5 %all-to-all-start.1 = ((bf16[12,8,8,462]{3,2,0,1:T(8,128)(2,1)}), bf16[12,8,8,462]{3,2,0,1:T(8,128)(2,1)}, u32[]{:S(2)}, u32[]{:S(2)}) async-start(bf16[12,8,8,462]{3,2,0,1:T(8,128)(2,1)} %copy.59), calls=%async_computation.1 | async-start | bytes 1572864 | tf_op jit(solution)/shard_map/all_to_all | solution.py:159
  180.1 28.9 %copy-start.14 = (bf16[1188,33]{0,1:T(8,128)(2,1)S(1)}, bf16[1188,33]{0,1:T(8,128)(2,1)}, u32[]{:S(2)}) copy-start(bf16[1188,33]{0,1:T(8,128)(2,1)} %convert_element_type.39) | copy-start | bytes 235228
  262.1 15.0 %copy-start.6 = (bf16[48,4,8,2,462]{4,0,3,2,1:T(8,128)(2,1)}, bf16[48,4,8,2,462]{4,0,3,2,1:T(8,128)(2,1)S(1)}, u32[]{:S(2)}) copy-start(bf16[48,4,8,2,462]{4,0,3,2,1:T(8,128)(2,1)S(1)} %broadcast_in_dim.42) | copy-start | bytes 8515588
  317.3 20.5 %copy-start.7 = (bf16[48,4,8,2,462]{4,0,3,2,1:T(8,128)(2,1)S(1)}, bf16[48,4,8,2,462]{4,0,3,2,1:T(8,128)(2,1)}, u32[]{:S(2)}) copy-start(bf16[48,4,8,2,462]{4,0,3,2,1:T(8,128)(2,1)} %copy-done.6) | copy-start | bytes 8515588
  334.7 9.9 %copy-start.3 = (bf16[48,4,16,924]{3,2,1,0:T(8,128)(2,1)}, bf16[48,4,16,924]{3,2,1,0:T(8,128)(2,1)S(1)}, u32[]{:S(2)}) copy-start(bf16[48,4,16,924]{3,2,1,0:T(8,128)(2,1)S(1)} %get-tuple-element.49) | copy-start | bytes 17031172
  362.9 29.7 %collective-permute-start.2 = (bf16[48,1,16,33]{3,2,1,0:T(8,128)(2,1)}, bf16[48,1,16,33]{3,2,1,0:T(8,128)(2,1)S(1)}, u32[]{:S(2)}, u32[]{:S(2)}) collective-permute-start(bf16[48,1,16,33]{3,2,1,0:T(8,128)(2,1)} %get-tuple-element.56), channel_id=1, source_target_pairs={{0,1},{1,2},{2,3},{4,5},{5,6},{6,7},{8,9},{9,10},{10,11},{12,13},{... | collective-permute-start | bytes 152072 | tf_op jit(solution)/shard_map/ppermute | solution.py:28
  364.2 28.4 %collective-permute-start.3 = (bf16[48,1,16,33]{3,2,1,0:T(8,128)(2,1)}, bf16[48,1,16,33]{3,2,1,0:T(8,128)(2,1)}, u32[]{:S(2)}, u32[]{:S(2)}) collective-permute-start(bf16[48,1,16,33]{3,2,1,0:T(8,128)(2,1)} %get-tuple-element.57), channel_id=1, source_target_pairs={{1,0},{2,1},{3,2},{5,4},{6,5},{7,6},{9,8},{10,9},{11,10},{13,12},{... | collective-permute-start | bytes 152072 | tf_op jit(solution)/shard_map/ppermute | solution.py:29
  385.7 144.1 %all-to-all-start = ((bf16[48,2,8,462]{3,2,1,0:T(8,128)(2,1)}), bf16[48,2,8,462]{3,2,1,0:T(8,128)(2,1)}, u32[]{:S(2)}, u32[]{:S(2)}) async-start(bf16[48,2,8,462]{3,2,1,0:T(8,128)(2,1)} %multiply_convert_fusion.4), calls=%async_computation | async-start | bytes 1572864 | tf_op jit(solution)/shard_map/all_to_all | solution.py:158
  392.2 260.6 %all-reduce.11.cloned.1.call-start = ((), (), s32[]{:S(2)}) async-start(), calls=%async_computation.2 | async-start | bytes 5185536 | tf_op jit(solution)/shard_map/psum | solution.py:223
  453.2 10.1 %copy-start.20 = (f32[891,132]{0,1:T(8,128)S(1)}, f32[891,132]{0,1:T(8,128)}, u32[]{:S(2)}) copy-start(f32[891,132]{0,1:T(8,128)} %param.15) | copy-start | bytes 1411348
  453.2 10.1 %copy-start.29 = (f32[891]{0:T(1024)S(1)}, f32[891]{0:T(1024)}, u32[]{:S(2)}) copy-start(f32[891]{0:T(1024)} %copy-done.28) | copy-start | bytes 10696
  453.2 10.1 %copy-start.31 = (f32[891]{0:T(1024)S(1)}, f32[891]{0:T(1024)}, u32[]{:S(2)}) copy-start(f32[891]{0:T(1024)} %copy-done.30) | copy-start | bytes 10696
  453.2 10.1 %copy-start.39 = (f32[891]{0:T(1024)S(1)}, f32[891]{0:T(1024)}, u32[]{:S(2)}) copy-start(f32[891]{0:T(1024)} %copy-done.38) | copy-start | bytes 10696
  514.8 14.4 %copy-start.27 = (f32[2,1947]{1,0:T(2,128)S(1)}, f32[2,1947]{1,0:T(2,128)}, u32[]{:S(2)}) copy-start(f32[2,1947]{1,0:T(2,128)} %param.13) | copy-start | bytes 46732
  514.8 14.4 %copy-start.40 = (f32[2,1947]{1,0:T(2,128)S(1)}, f32[2,1947]{1,0:T(2,128)}, u32[]{:S(2)}) copy-start(f32[2,1947]{1,0:T(2,128)} %param.14) | copy-start | bytes 46732
  514.8 138.0 %copy-start.8 = (f32[924,462]{1,0:T(8,128)S(1)}, f32[924,462]{1,0:T(8,128)}, u32[]{:S(2)}) copy-start(f32[924,462]{1,0:T(8,128)} %param.20) | copy-start | bytes 5122660
  (26 other events, 104.8 us)
Sparse Core Ops, SparseCore 0:
  514.9 137.8 all-reduce.10
where the time goes:
time: 738 us; the launch traced here: 729 us
  blocking collectives  244 us (33%)
  matrix products  134 us (18%)
  waiting for transfers between devices  121 us (16%)
  local copies, waits for them, and re-layouts  101 us (14%)
  other arithmetic  92.2 us (12%)
  starting transfers between devices  19.1 us (3%)
  between operations  18 us (2%)
    psum x1, waiting for transfers between devices, per_device(): lax.psum((grad_w_first, grad_w_taps, grad_w_last), ('batch', 'rows'))  121 us
    psum x2, blocking collectives, per_device(): lax.psum((local_sum, local_square), ('batch', 'rows'))  81 us
    psum x1, blocking collectives, per_device(): lax.psum((local_sum, local_square, jnp.sum(valid_cells)), ('batch', 'rows'))  42.3 us
    psum x1, blocking collectives, per_device(): lax.psum((middle_gain_local, middle_shift_local), ('batch', 'rows'))  40.8 us
    psum x1, blocking collectives, per_device(): lax.psum((last_gain_local, last_shift_local), ('batch', 'rows'))  40.1 us
    psum x1, blocking collectives, per_device(): lax.psum((first_gain_local, first_shift_local), ('batch', 'rows'))  40.1 us
    another operation x2, local copies, waits for them, and re-layouts, forward_taps(): jnp.stack(pieces, axis=-1)  32.5 us
    reshape x1, local copies, waits for them, and re-layouts, forward_taps(): jnp.stack(pieces, axis=-1)  28.9 us
  transfers between devices with their start and end apart: 7, of which 1 were waited for; matrix products, arithmetic and copies ran while one was open for 24% of the time, Pallas kernels for 0%

commit v1 on v0

v1 whole, which is shorter than its diff:
```python
import functools

import jax
import jax.numpy as jnp
from jax import lax
from jax.experimental import pallas as pl
from jax.experimental.pallas import tpu as pltpu
from jax.sharding import PartitionSpec as P

SMALL = 12
NS_STEPS = 5
EPSILON = 1e-05
MOMENTUM_DECAY = 0.9
MUON_RATE = 0.5
NORM_RATE = 1.0
QUINTIC_A = 3.4445
QUINTIC_B = -4.775
QUINTIC_C = 2.0315
TINY = 1e-07
F32 = jnp.float32
BF16 = jnp.bfloat16
MESH = pl.DeviceIdType.MESH
LANES = 128
TILE_IMGS = 4
VMEM_BYTES = 62 * 1024 * 1024


def dot(a, b, ca, cb):
    return lax.dot_general(a, b, (((ca,), (cb,)), ((), ())), preferred_element_type=F32)


def split(a):
    high = a.astype(BF16)
    return high, (a - high.astype(F32)).astype(BF16)


def round_up(value, step):
    return -(-value // step) * step


def fold_rows(value):
    rows, cols = value.shape
    return jnp.sum(value.reshape(rows // 8, 8, cols), axis=0)


def lane_tiles(total):
    return [(j, min(LANES, total - j)) for j in range(0, total, LANES)]


def lane_blocks(total):
    return [(j, min(2 * LANES, total - j)) for j in range(0, total, 2 * LANES)]


def zeros_for(pieces):
    return tuple(jnp.zeros((8, w), F32) for _, w in pieces)


def pack_row(slots, r, top, row):
    for k, (j, w) in enumerate(lane_tiles(row.shape[1])):
        slots[r, top + k : top + k + 1, 0:w] = row[:, j : j + w]


def unpack_row(total, top, size):
    return jnp.concatenate([total[top + k : top + k + 1, 0:w] for k, (_, w) in enumerate(lane_tiles(size))], axis=1)


def row_sum(value):
    return jnp.sum(value, axis=0, keepdims=True)


class VectorReduce:
    def __init__(self, place, counts, refs):
        self.r, self.b = place
        self.rows, self.batch = counts
        self.row_slots, self.batch_slots, self.row_sems, self.batch_sems = refs

    def copies(self, axis, me, count, slots, sems):
        made = []
        for step in range(1, count):
            peer = lax.rem(me + step, count)
            made.append(
                pltpu.make_async_remote_copy(
                    src_ref=slots.at[me],
                    dst_ref=slots.at[me],
                    send_sem=sems.at[0, step],
                    recv_sem=sems.at[1, step],
                    device_id={axis: peer},
                    device_id_type=MESH,
                )
            )
        return made

    def start(self):
        self.first = self.copies("rows", self.r, self.rows, self.row_slots, self.row_sems)
        for copy in self.first:
            copy.start()

    def middle(self):
        for copy in self.first:
            copy.wait_recv()
        total = self.row_slots[0]
        for j in range(1, self.rows):
            total = total + self.row_slots[j]
        self.batch_slots[self.b] = total
        self.second = self.copies("batch", self.b, self.batch, self.batch_slots, self.batch_sems)
        for copy in self.second:
            copy.start()

    def finish(self):
        for copy in self.second:
            copy.wait_recv()
        total = self.batch_slots[0]
        for j in range(1, self.batch):
            total = total + self.batch_slots[j]
        for copy in self.first + self.second:
            copy.wait_send()
        return total


class BlockReduce:
    def __init__(self, place, counts, refs):
        self.r, self.b = place
        self.batch = counts[1]
        self.local, self.out_a, self.in_a, self.in_b, self.in_c, self.full, self.sems = refs
        self.length = self.local.shape[0]
        self.out_b = self.out_a.at[pl.ds(0, self.length // 4)]
        self.out_c = self.out_a.at[pl.ds(self.length // 4, self.length // 4)]
        self.chunk = self.length // (4 * self.batch)
        self.low, self.high = lax.rem(self.r, 2), lax.div(self.r, 2)
        self.near = self.r + 1 - 2 * self.low
        self.far = self.r + 2 - 4 * self.high

    def each(self, count, body):
        step = 16
        for size in (256, 128, 64, 32):
            if count % size == 0:
                step = size
                break

        def run(i, carry):
            body(pl.multiple_of(i * step, 16), step)
            return carry

        lax.fori_loop(0, count // step, run, 0)

    def copy(self, src, dst, axis, peer, slot):
        return pltpu.make_async_remote_copy(
            src_ref=src,
            dst_ref=dst,
            send_sem=self.sems.at[0, slot],
            recv_sem=self.sems.at[1, slot],
            device_id={axis: peer},
            device_id_type=MESH,
        )

    def at(self, start, size):
        return pl.ds(pl.multiple_of(start, 16), size)

    def start(self):
        half = self.length // 2
        other = (1 - self.low) * half

        def body(i, n):
            self.out_a[self.at(i, n)] = self.local[self.at(other + i, n)].astype(BF16)

        self.each(half, body)
        self.a = self.copy(self.out_a, self.in_a, "rows", self.near, 0)
        self.a.start()

    def step_b(self):
        quarter = self.length // 4
        self.a.wait()
        other = (1 - self.high) * quarter
        mine = self.low * 2 * quarter

        def body(i, n):
            total = self.local[self.at(mine + other + i, n)] + self.in_a[self.at(other + i, n)].astype(F32)
            self.out_b[self.at(i, n)] = total.astype(BF16)

        self.each(quarter, body)
        self.b_copy = self.copy(self.out_b, self.in_b, "rows", self.far, 1)
        self.b_copy.start()

    def step_c(self):
        quarter = self.length // 4
        self.b_copy.wait()
        mine = self.low * 2 * quarter + self.high * quarter

        def body(i, n):
            total = self.local[self.at(mine + i, n)] + self.in_a[self.at(self.high * quarter + i, n)].astype(F32)
            total = total + self.in_b[self.at(i, n)].astype(F32)
            self.local[self.at(mine + i, n)] = total
            self.out_c[self.at(i, n)] = total.astype(BF16)

        self.each(quarter, body)
        self.c = []
        for step in range(1, self.batch):
            peer = lax.rem(self.b + step, self.batch)
            piece = self.out_c.at[self.at(peer * self.chunk, self.chunk)]
            self.c.append(self.copy(piece, self.in_c.at[step], "batch", peer, 1 + step))
        for copy in self.c:
            copy.start()

    def step_d(self):
        quarter = self.length // 4
        for copy in self.c:
            copy.wait()
        mine = self.low * 2 * quarter + self.high * quarter + self.b * self.chunk

        def body(i, n):
            total = self.local[self.at(mine + i, n)]
            for step in range(1, self.batch):
                total = total + self.in_c[step, self.at(i, n)].astype(F32)
            self.full[self.at(mine + i, n)] = total.astype(BF16)

        self.each(self.chunk, body)
        piece = self.full.at[self.at(mine, self.chunk)]
        self.d = []
        for step in range(1, self.batch):
            peer = lax.rem(self.b + step, self.batch)
            self.d.append(self.copy(piece, piece, "batch", peer, self.batch + step))
        for copy in self.d:
            copy.start()

    def step_e(self):
        quarter = self.length // 4
        for copy in self.d:
            copy.wait()
        self.e_copy().start()

    def e_copy(self):
        quarter = self.length // 4
        piece = self.full.at[self.at(self.low * 2 * quarter + self.high * quarter, quarter)]
        return self.copy(piece, piece, "rows", self.far, 2 * self.batch)

    def step_f(self):
        half = self.length // 2
        self.e_copy().wait()
        piece = self.full.at[self.at(self.low * half, half)]
        self.f = self.copy(piece, piece, "rows", self.near, 2 * self.batch + 1)
        self.f.start()

    def finish(self):
        self.f.wait()

    @staticmethod
    def scratch(length, batch):
        shapes = (length // 2, length // 2, length // 4)
        return (
            [pltpu.VMEM((length, LANES), F32)]
            + [pltpu.VMEM((n, LANES), BF16) for n in shapes]
            + [
                pltpu.VMEM((batch, length // (4 * batch), LANES), BF16),
                pltpu.VMEM((length, LANES), BF16),
                pltpu.SemaphoreType.DMA((2, 2 * batch + 2)),
            ]
        )


def band_kernel(dims, flags, x_hbm, cot_hbm, params, wf_hbm, wg_hbm, wl_hbm, *rest):
    (rows, batch, images, c0, bot, gr, trans, own) = dims
    cat = c0 + gr
    (ig_hbm, pool_hbm, stats, sum_a, sum_c) = rest[:5]
    rest = list(rest[5:])

    def take(n):
        taken = rest[:n]
        del rest[:n]
        return taken

    (xv, av, sv, mv, pmv, px, tin, ting, ev, eg, cotv) = take(11)
    (bnv, a2v, s2v, gv, ggv, gmv) = take(6)
    (wlf, wlb, wlg, wff, wfb, wfn, wgf, wft, wfm, wbm, pmat, umat, cvec, poolv, gt) = take(15)
    (x_sems, io_sems, cot_sems, halo_sems, gg_sems, pool_sems) = take(6)
    small = [take(4) for _ in range(4)]
    small.append(small[0][:2] + take(2))
    small.append(take(4))
    big = [take(7) for _ in range(2)]
    up = take(1)[0]
    local_b = local_c = big[1][0]

    r, b = lax.axis_index("rows"), lax.axis_index("batch")
    place, counts = (r, b), (rows, batch)
    n_pix, n_cell = images * 64, images * 16
    tiles = images // TILE_IMGS
    tp, tc = TILE_IMGS * 64, TILE_IMGS * 16

    w_copies = [
        pltpu.make_async_copy(wf_hbm, wff, io_sems.at[0]),
        pltpu.make_async_copy(wg_hbm, wgf, io_sems.at[1]),
        pltpu.make_async_copy(wl_hbm, wlf, io_sems.at[2]),
    ]
    w_copies[1].start()
    x_copies = [
        pltpu.make_async_copy(x_hbm.at[pl.ds(pl.multiple_of(t * tp, tp), tp)], xv.at[pl.ds(pl.multiple_of(t * tp, tp), tp)], x_sems.at[t]) for t in range(tiles)
    ]
    for copy in x_copies:
        copy.start()
    w_copies[0].start()
    w_copies[2].start()
    cot_own = pltpu.make_async_copy(
        cot_hbm.at[:, pl.ds(pl.multiple_of(r * 16, 16), 16)], cotv.at[pl.ds(r * own, own)], io_sems.at[3]
    )
    cot_own.start()
    barrier = pltpu.get_barrier_semaphore()
    for axis, me, count in (("rows", r, rows), ("batch", b, batch)):
        for step in range(1, count):
            pl.semaphore_signal(barrier, inc=1, device_id={axis: lax.rem(me + step, count)}, device_id_type=MESH)

    a_id = lax.broadcasted_iota(jnp.int32, (tc, tp), 0)
    b_id = lax.broadcasted_iota(jnp.int32, (tc, tp), 1)
    hit = (a_id // 8 == b_id // 32) & (a_id % 8 == (b_id % 16) // 2)
    pmat[...] = jnp.where(hit, 1.0, 0.0).astype(BF16)
    a_id = lax.broadcasted_iota(jnp.int32, (tp, tc), 1)
    b_id = lax.broadcasted_iota(jnp.int32, (tp, tc), 0)
    hit = (a_id // 8 == b_id // 32) & (a_id % 8 == (b_id % 16) // 2)
    umat[...] = jnp.where(hit, 1.0, 0.0).astype(BF16)

    pix = lax.broadcasted_iota(jnp.int32, (64, 1), 0)
    inside = jnp.where((r * 4 + pix // 16 < SMALL) & (pix % 16 < SMALL), 1.0, 0.0)
    cell = lax.broadcasted_iota(jnp.int32, (16, 1), 0)
    inside_cell = jnp.where((r * 4 + cell // 8 * 2 < SMALL) & (cell % 8 * 2 < SMALL), 1.0, 0.0)
    inside_above = jnp.where((r * 4 - 1 < SMALL) & (cell < SMALL), 1.0, 0.0)
    inside_below = jnp.where((r * 4 + 4 < SMALL) & (cell < SMALL), 1.0, 0.0)
    have_above = jnp.where(r > 0, 1.0, 0.0)
    have_below = jnp.where(r < rows - 1, 1.0, 0.0)
    inside_count = jnp.clip(SMALL - r * 4, 0, 4) * SMALL

    copy_id = lax.broadcasted_iota(jnp.int32, (LANES, gr), 0)
    lane_id = lax.broadcasted_iota(jnp.int32, (LANES, gr), 1)
    spread = jnp.where((copy_id % gr == lane_id) & (copy_id < 3 * gr), 1.0, 0.0).astype(BF16)
    w_copies[1].wait()
    wgb = wgf[...].astype(BF16)
    gap = lax.broadcasted_iota(jnp.int32, (9 * bot, bot), 0) - 9 * lax.broadcasted_iota(jnp.int32, (9 * bot, bot), 1)
    wft[...] = jnp.zeros_like(wft)
    for dh in range(3):
        for dw in range(3):
            pick = jnp.where(gap == 3 * dh + dw, 1.0, 0.0).astype(BF16)
            tap = dot(wgb, pick, 1, 0)
            for c in range(3):
                wft[dh, LANES * dw + gr * c : LANES * dw + gr * (c + 1), :] = tap
            wft[3, LANES * dw + gr * dh : LANES * dw + gr * (dh + 1), :] = tap
    for dh in range(3):
        wfm[dh] = wft[dh].T.astype(BF16)
    wbm[...] = wft[3].astype(BF16)


    tiles_c0, blocks_c0 = lane_tiles(c0), lane_blocks(c0)

    def sums_body(t, carry):
        acc, acc2, count = carry
        pltpu.make_async_copy(x_hbm.at[pl.ds(pl.multiple_of(t * tp, tp), tp)], xv.at[pl.ds(pl.multiple_of(t * tp, tp), tp)], x_sems.at[t]).wait()
        for q in range(TILE_IMGS):
            img = t * TILE_IMGS + q
            is_small = flags[img] > 0
            count = count + jnp.where(is_small, inside_count, 64)
            mask = jnp.where(is_small, inside, 1.0)
            mv[pl.ds(img * 64, 64), :] = jnp.broadcast_to(mask, (64, LANES))
            pmv[pl.ds(img * 16, 16), :] = jnp.broadcast_to(jnp.where(is_small, inside_cell, 1.0), (16, LANES))
        squares, firsts = [], []
        for k, (j, w) in enumerate(tiles_c0):
            total = acc2[k]
            for i in range(0, tp, 32):
                x = xv[pl.ds(pl.multiple_of(t * tp + i, 32), 32), j : j + w].astype(F32)
                total = total + fold_rows(x * x * mv[pl.ds(pl.multiple_of(t * tp + i, 32), 32), 0:w])
            squares.append(total)
        for k, (j, w) in enumerate(blocks_c0):
            cells = dot(pmat[...], xv[pl.ds(pl.multiple_of(t * tp, tp), tp), j : j + w], 1, 0) * pmv[pl.ds(pl.multiple_of(t * tc, tc), tc), 0:1]
            px[pl.ds(pl.multiple_of(t * tc, tc), tc), j : j + w] = cells
            firsts.append(acc[k] + fold_rows(cells))
        return tuple(firsts), tuple(squares), count

    acc, acc2, count = lax.fori_loop(0, tiles, sums_body, (zeros_for(blocks_c0), zeros_for(tiles_c0), jnp.int32(0)))
    acc, acc2 = jnp.concatenate(acc, axis=1), jnp.concatenate(acc2, axis=1)
    red1 = VectorReduce(place, counts, small[0])
    slot = small[0][0]
    span = len(tiles_c0)
    pack_row(slot, r, 0, row_sum(acc))
    pack_row(slot, r, span, row_sum(acc2))
    slot[r, 2 * span : 2 * span + 1, :] = jnp.full((1, LANES), count.astype(F32))
    pl.semaphore_wait(barrier, rows - 1 + batch - 1)
    red1.start()

    w_copies[0].wait()
    w_copies[2].wait()
    wfb[...] = wff[...].astype(BF16)
    wfn[...] = wff[...].T.astype(BF16)
    wlb[...] = wlf[...].astype(BF16)
    red1.middle()
    cot_copies = []
    for step in range(1, rows):
        peer = lax.rem(r + step, rows)
        cot_copies.append(
            pltpu.make_async_remote_copy(
                src_ref=cot_hbm.at[:, pl.ds(pl.multiple_of(peer * 16, 16), 16)],
                dst_ref=cotv.at[pl.ds(r * own, own)],
                send_sem=cot_sems.at[0, step],
                recv_sem=cot_sems.at[1, step],
                device_id={"rows": peer},
                device_id_type=MESH,
            )
        )
    for copy in cot_copies:
        copy.start()

    wlg[...] = dot(spread, wlf[c0:cat, :].astype(BF16), 1, 0).astype(BF16)
    total = red1.finish()
    count_all = total[2 * span : 2 * span + 1, 0:1]
    per = 1.0 / count_all
    mean1 = unpack_row(total, 0, c0) * per
    inv1 = lax.rsqrt(unpack_row(total, span, c0) * per - mean1 * mean1 + EPSILON)
    gain1, shift1 = params[0:1, 0:c0], params[1:2, 0:c0]
    gain2, shift2 = params[0:1, c0 : c0 + bot], params[1:2, c0 : c0 + bot]
    gain3, shift3 = params[0:1, c0 + bot : 2 * c0 + bot], params[1:2, c0 + bot : 2 * c0 + bot]
    gaing, shiftg = params[0:1, 2 * c0 + bot :], params[1:2, 2 * c0 + bot :]
    half_a = 0.5 * gain1 * inv1
    half_b = 0.5 * shift1 - mean1 * half_a
    trans_a = gain3 * inv1
    trans_b = shift3 - mean1 * trans_a
    cvec[0:1, 0:c0] = half_a
    cvec[1:2, 0:c0] = half_b
    cvec[2:3, 0:c0] = 0.25 * trans_a
    cvec[3:4, 0:c0] = trans_b
    cvec[4:5, 0:c0] = mean1
    cvec[5:6, 0:c0] = inv1
    cvec[6:7, 0:c0] = gain1 * inv1
    cvec[7:8, 0:c0] = trans_a

    def first_act(t):
        for j, w in tiles_c0:
            cols = slice(j, j + w)
            scale, shift = cvec[0:1, cols], cvec[1:2, cols]
            for i in range(0, tp, 32):
                at = pl.ds(pl.multiple_of(t * tp + i, 32), 32)
                h = xv[at, cols].astype(F32) * scale + shift
                th = jnp.tanh(h)
                ht = h * th
                av[at, cols] = (h + ht).astype(BF16)
                sv[at, cols] = ((1.0 + th) * (1.0 + (h - ht))).astype(BF16)
            scale, shift = cvec[2:3, cols], cvec[3:4, cols]
            for i in range(0, tc, 32):
                ct = pl.ds(pl.multiple_of(t * tc + i, 32), 32)
                tin[ct, cols] = (px[ct, cols] * scale + pmv[ct, 0:w] * shift).astype(BF16)

    def first_product(t, carry):
        acc, acc2 = carry
        at = pl.ds(pl.multiple_of(t * tp, tp), tp)
        value = dot(av[at, :], wfn[...], 1, 0) * mv[at, 0:1]
        bnv[pl.ds(t * TILE_IMGS, TILE_IMGS)] = value.reshape(TILE_IMGS, 4, 16, bot)
        return acc + fold_rows(value), acc2 + fold_rows(value * value)

    def first_body(t, carry):
        carry = first_product(t - 1, carry)
        first_act(t)
        return carry

    zero = jnp.zeros((8, bot), F32)
    first_act(0)
    acc, acc2 = first_product(tiles - 1, lax.fori_loop(1, tiles, first_body, (zero, zero)))
    red2 = VectorReduce(place, counts, small[1])
    slot = small[1][0]
    pack_row(slot, r, 0, row_sum(acc))
    pack_row(slot, r, 2, row_sum(acc2))
    red2.start()
    a2v[:, 1] = bnv[:, 0].astype(BF16)
    a2v[:, 4] = bnv[:, 3].astype(BF16)

    def edge_copy(ref, sems, side, send):
        return pltpu.make_async_remote_copy(
            src_ref=ref.at[:, 1 + 3 * side],
            dst_ref=ref.at[:, 5 - 5 * side if send else 5 * side],
            send_sem=sems.at[0, side],
            recv_sem=sems.at[1, 1 - side if send else side],
            device_id={"rows": lax.rem(r + rows - 1 + 2 * side, rows)},
            device_id_type=MESH,
        )

    def on_edges(action):
        pl.when(r > 0)(lambda: action(0))
        pl.when(r < rows - 1)(lambda: action(1))

    on_edges(lambda side: edge_copy(a2v, halo_sems, side, True).start())
    cot_own.wait()
    for copy in cot_copies:
        copy.wait()
    red2.middle()

    cot_all = cotv[...].reshape(n_cell, trans)
    eg[...] = dot(cot_all, wlg[...], 1, 1)
    acc_e, acc_ex = [], []
    for j, w in blocks_c0:
        value = dot(cot_all, wlb[j : j + w, :], 1, 1)
        ev[:, j : j + w] = value
        total, total2 = jnp.zeros((8, w), F32), jnp.zeros((8, w), F32)
        for i in range(0, n_cell, 32):
            piece = value[i : i + 32]
            total = total + fold_rows(piece * pmv[i : i + 32, 0:1])
            total2 = total2 + fold_rows(piece * px[i : i + 32, j : j + w])
        acc_e.append(total)
        acc_ex.append(total2)
    acc_e, acc_ex = jnp.concatenate(acc_e, axis=1), jnp.concatenate(acc_ex, axis=1)
    red6 = VectorReduce(place, counts, small[5])
    pack_row(small[5][0], r, 0, row_sum(acc_e))
    pack_row(small[5][0], r, span, row_sum(acc_ex))
    red_a = BlockReduce(place, counts, big[0])
    local_a = big[0][0]
    stride_a = round_up(c0, 16)
    step_rows = 256
    for i in range(0, c0, step_rows):
        n = min(step_rows, c0 - i)
        value = dot(tin[:, i : i + n], cot_all, 0, 0)
        for j in range(0, trans, LANES):
            w = min(LANES, trans - j)
            local_a[j // LANES * stride_a + i : j // LANES * stride_a + i + n, 0:w] = value[:, j : j + w]

    total = red2.finish()
    mean2 = unpack_row(total, 0, bot) * per
    inv2 = lax.rsqrt(unpack_row(total, 2, bot) * per - mean2 * mean2 + EPSILON)
    half_a2 = 0.5 * gain2 * inv2
    half_b2 = 0.5 * shift2 - mean2 * half_a2
    red6.start()
    red_a.start()

    on_edges(lambda side: edge_copy(a2v, halo_sems, side, True).wait_send())

    def middle_body(t, carry):
        imgs = pl.ds(t * TILE_IMGS, TILE_IMGS)
        at = pl.ds(pl.multiple_of(t * tp, tp), tp)
        h = bnv[imgs].reshape(tp, bot) * half_a2 + half_b2
        th = jnp.tanh(h)
        ht = h * th
        mask = mv[at, 0:1]
        a2v[imgs, 1:5] = ((h + ht) * mask).astype(BF16).reshape(TILE_IMGS, 4, 16, bot)
        s2v[at, :] = ((1.0 + th) * (1.0 + (h - ht)) * (0.5 * mask)).astype(BF16)
        return carry

    lax.fori_loop(0, tiles, middle_body, 0)

    on_edges(lambda side: edge_copy(a2v, halo_sems, side, False).wait_recv())
    for side, row, fits, have in ((0, 0, inside_above, have_above), (1, 5, inside_below, have_below)):

        def edge_body(t, carry, side=side, row=row, fits=fits, have=have):
            size = 16
            imgs = pl.ds(pl.multiple_of(t * size, size), size)
            h = a2v[imgs, row].astype(F32).reshape(size * 16, bot) * half_a2 + half_b2
            value = h + h * jnp.tanh(h)
            mask = [jnp.where(flags[t * size + q] > 0, fits, 1.0) * have for q in range(size)]
            value = jnp.where(jnp.concatenate(mask, axis=0) > 0.0, value, 0.0)
            a2v[imgs, row] = value.astype(BF16).reshape(size, 16, bot)
            return carry

        lax.fori_loop(0, images // 16, edge_body, 0)
    red_a.step_b()
    red6.middle()

    col = lax.broadcasted_iota(jnp.int32, (tp, 1), 0) % 16
    not_first, not_last = jnp.where(col > 0, 1.0, 0.0), jnp.where(col < 15, 1.0, 0.0)

    def growth_body(t, carry):
        acc, acc2, acc_e, acc_eg = carry
        imgs = pl.ds(t * TILE_IMGS, TILE_IMGS)
        at, ct = pl.ds(pl.multiple_of(t * tp, tp), tp), pl.ds(pl.multiple_of(t * tc, tc), tc)
        z = dot(a2v[imgs, 0:4].reshape(tp, bot), wfm[0], 1, 0)
        z = z + dot(a2v[imgs, 1:5].reshape(tp, bot), wfm[1], 1, 0)
        z = z + dot(a2v[imgs, 2:6].reshape(tp, bot), wfm[2], 1, 0)
        left = pltpu.roll(z[:, 0:LANES], 1, 0) * not_first
        right = pltpu.roll(z[:, 2 * LANES :], tp - 1, 0) * not_last
        g = left + z[:, LANES : 2 * LANES] + right
        gv[at, :] = g
        gm = g * mv[at, :]
        high, low = split(gm)
        pg = dot(pmat[...], high, 1, 0) + dot(pmat[...], low, 1, 0)
        gt[ct, :] = pg
        e = eg[ct, :]
        return acc + fold_rows(pg), acc2 + fold_rows(gm * g), acc_e + fold_rows(e * pmv[ct, :]), acc_eg + fold_rows(e * pg)

    zero = jnp.zeros((8, LANES), F32)
    sums = lax.fori_loop(0, tiles, growth_body, (zero,) * 4)
    red3 = VectorReduce(place, counts, small[2])
    slot = small[2][0]
    for j in range(4):
        slot[r, j : j + 1, :] = row_sum(sums[j])
    red3.start()

    def part_body(t, carry):
        ct = pl.ds(pl.multiple_of(t * 256, 256), 256)
        px[ct, 0:trans] = dot(tin[ct, :], wlb[0:c0, :], 1, 0)
        return carry

    lax.fori_loop(0, n_cell // 256, part_body, 0)
    red3.middle()
    red_a.step_c()
    poolv[...] = jnp.zeros_like(poolv)
    for c in range(3):
        poolv[0:1, gr * c : gr * (c + 1)] = gaing
        poolv[1:2, gr * c : gr * (c + 1)] = shiftg
    gain_g, shift_g = poolv[0:1, :], poolv[1:2, :]
    total = red3.finish()
    mean_g = total[0:1, :] * per
    inv_g = lax.rsqrt(total[1:2, :] * per - mean_g * mean_g + EPSILON)
    shift_grad_g = total[2:3, :]
    gain_grad_g = inv_g * (0.25 * total[3:4, :] - mean_g * shift_grad_g)
    scale_g = gain_g * inv_g
    slope_g = scale_g * gain_grad_g * inv_g * per
    const_g = slope_g * mean_g - scale_g * shift_grad_g * per
    off_g = shift_g - mean_g * scale_g

    def grad_body(t, carry):
        imgs = pl.ds(t * TILE_IMGS, TILE_IMGS)
        at, ct = pl.ds(pl.multiple_of(t * tp, tp), tp), pl.ds(pl.multiple_of(t * tc, tc), tc)
        high, low = split(eg[ct, :] * (0.25 * scale_g) + const_g)
        wide = dot(umat[...], high, 1, 0) + dot(umat[...], low, 1, 0)
        gg = (wide - gv[at, :] * slope_g) * mv[at, :]
        ggv[imgs, 1:5] = gg.astype(BF16).reshape(TILE_IMGS, 4, 16, LANES)
        ting[ct, :] = (gt[ct, :] * (0.25 * scale_g) + pmv[ct, :] * off_g).astype(BF16)
        return carry

    lax.fori_loop(0, tiles, grad_body, 0)

    on_edges(lambda side: edge_copy(ggv, gg_sems, side, True).start())

    @pl.when(r == 0)
    def _():
        ggv[:, 0] = jnp.zeros((images, 16, LANES), BF16)

    @pl.when(r == rows - 1)
    def _():
        ggv[:, 5] = jnp.zeros((images, 16, LANES), BF16)

    lane = lax.broadcasted_iota(jnp.int32, (1, LANES), 1)

    def pool_body(t, carry):
        ct = pl.ds(pl.multiple_of(t * 256, 256), 256)
        own_g = jnp.where(lane < gr, ting[ct, :].astype(F32), 0.0).astype(BF16)
        value = px[ct, 0:trans] + dot(own_g, wlg[...], 1, 0)
        hpool[pl.ds(t * 16, 16)] = value.astype(BF16).reshape(16, 16, trans)
        return carry

    hpool = take(1)[0]
    lax.fori_loop(0, n_cell // 256, pool_body, 0)
    pool_copies = []
    for step in range(1, rows):
        peer = lax.rem(r + step, rows)
        pool_copies.append(
            pltpu.make_async_remote_copy(
                src_ref=hpool.at[pl.ds(peer * own, own)],
                dst_ref=cotv.at[pl.ds(r * own, own)],
                send_sem=pool_sems.at[0, step],
                recv_sem=pool_sems.at[1, step],
                device_id={"rows": peer},
                device_id_type=MESH,
            )
        )
    red_a.step_d()
    red_c = BlockReduce(place, counts, big[1])
    local_c[...] = jnp.zeros_like(local_c)
    base_c = len(tiles_c0) * round_up(bot, 8)
    stride_g = round_up(gr, 8)
    value = dot(ting[...], cot_all, 0, 0)
    for j in range(0, trans, LANES):
        w = min(LANES, trans - j)
        top = base_c + j // LANES * stride_g
        local_c[top : top + gr, 0:w] = value[0:gr, j : j + w]
    base_taps = base_c + -(-trans // LANES) * stride_g

    on_edges(lambda side: edge_copy(ggv, gg_sems, side, True).wait_send())
    on_edges(lambda side: edge_copy(ggv, gg_sems, side, False).wait_recv())
    lanes_all = lax.broadcasted_iota(jnp.int32, (tp, LANES), 1)
    wft[0] = jnp.zeros(wft.shape[1:], F32)

    def conv_body(t, carry):
        acc, acc2 = carry
        imgs = pl.ds(t * TILE_IMGS, TILE_IMGS)
        at = pl.ds(pl.multiple_of(t * tp, tp), tp)
        above = ggv[imgs, 0:4].reshape(tp, LANES).astype(F32)
        here = ggv[imgs, 1:5].reshape(tp, LANES).astype(F32)
        below = ggv[imgs, 2:6].reshape(tp, LANES).astype(F32)
        mixed = jnp.where(lanes_all < gr, below, jnp.where(lanes_all < 2 * gr, here, jnp.where(lanes_all < 3 * gr, above, 0.0)))
        from_right = pltpu.roll(mixed, tp - 1, 0) * not_last
        from_left = pltpu.roll(mixed, 1, 0) * not_first
        patch = jnp.concatenate([from_right, mixed, from_left], axis=1).astype(BF16)
        gm = dot(patch, wbm[...], 1, 0) * s2v[at, :].astype(F32)
        gmv[at, :] = gm
        wft[0] += dot(patch, a2v[imgs, 1:5].reshape(tp, bot), 0, 0)
        hat = bnv[imgs].reshape(tp, bot) - mean2
        return acc + fold_rows(gm), acc2 + fold_rows(gm * hat)

    zero = jnp.zeros((8, bot), F32)
    acc, acc2 = lax.fori_loop(0, tiles, conv_body, (zero, zero))
    red4 = VectorReduce(place, counts, small[3])
    slot = small[3][0]
    pack_row(slot, r, 0, row_sum(acc))
    pack_row(slot, r, 2, row_sum(acc2))
    red4.start()
    red4.middle()
    for copy in pool_copies:
        copy.start()
    pool_own = pltpu.make_async_copy(
        hpool.at[pl.ds(r * own, own)], pool_hbm.at[:, pl.ds(pl.multiple_of(r * 16, 16), 16)], io_sems.at[4]
    )
    pool_own.start()
    red_a.step_e()
    gap = lax.broadcasted_iota(jnp.int32, (bot, 9 * bot), 1) - 9 * lax.broadcasted_iota(jnp.int32, (bot, 9 * bot), 0)
    value = jnp.zeros((gr, 9 * bot), F32)
    for dh in range(3):
        for dw in range(3):
            pick = jnp.where(gap == 3 * dh + dw, 1.0, 0.0).astype(BF16)
            tap = wft[0, LANES * dw + gr * dh : LANES * dw + gr * (dh + 1), :]
            high, low = split(tap)
            value = value + (dot(high, pick, 1, 0) + dot(low, pick, 1, 0))
    for j in range(0, 9 * bot, LANES):
        w = min(LANES, 9 * bot - j)
        top = base_taps + j // LANES * stride_g
        local_c[top : top + gr, 0:w] = value[:, j : j + w]
    total = red4.finish()
    shift_grad2 = unpack_row(total, 0, bot)
    gain_grad2 = inv2 * unpack_row(total, 2, bot)
    scale2 = gain2 * inv2
    slope2 = scale2 * gain_grad2 * inv2 * per
    const2 = scale2 * shift_grad2 * per - slope2 * mean2

    stride_f = round_up(bot, 8)
    blocks = -(-c0 // LANES)

    def bottleneck_body(t, carry):
        imgs = pl.ds(t * TILE_IMGS, TILE_IMGS)
        at = pl.ds(pl.multiple_of(t * tp, tp), tp)
        bn = bnv[imgs].reshape(tp, bot)
        gb = ((gmv[at, :] * scale2 - bn * slope2 - const2) * mv[at, 0:1]).astype(BF16)
        s2v[at, :] = gb
        grad = dot(gb, av[at, :], 0, 0)
        for k, (j, w) in enumerate(tiles_c0):
            local_b[k * stride_f : k * stride_f + bot, 0:w] += grad[:, j : j + w]
        return carry

    lax.fori_loop(0, tiles, bottleneck_body, 0)
    red_c.start()

    def back_body(t, carry):
        acc, acc2 = carry
        at = pl.ds(pl.multiple_of(t * tp, tp), tp)
        gb = s2v[at, :]
        sums, cross = [], []
        for k, (j, w) in enumerate(blocks_c0):
            cols = slice(j, j + w)
            value = dot(gb, wfb[:, cols], 1, 0)
            total, total2 = acc[k], acc2[k]
            for i in range(0, tp, 32):
                part = pl.ds(pl.multiple_of(t * tp + i, 32), 32)
                gf = value[i : i + 32] * sv[part, cols].astype(F32)
                av[part, cols] = gf.astype(BF16)
                total = total + fold_rows(gf)
                total2 = total2 + fold_rows(gf * xv[part, cols].astype(F32))
            sums.append(total)
            cross.append(total2)
        return tuple(sums), tuple(cross)

    zero = zeros_for(blocks_c0)
    sums = lax.fori_loop(0, tiles // 2, back_body, (zero, zero))
    red_c.step_b()
    sums = lax.fori_loop(tiles // 2, tiles, back_body, sums)
    acc, acc2 = jnp.concatenate(sums[0], axis=1), jnp.concatenate(sums[1], axis=1)
    red5 = VectorReduce(place, counts, small[4])
    pack_row(small[4][0], r, 0, row_sum(acc))
    pack_row(small[4][0], r, span, row_sum(acc2))
    red5.start()
    red_c.step_c()
    cvec[0:1, 0:c0] = 0.25 * cvec[7:8, 0:c0]
    cvec[2:3, 0:c0] = 0.5 * cvec[6:7, 0:c0]

    def part_grad(t, carry):
        for q in range(TILE_IMGS):
            img = t * TILE_IMGS + q
            for j, w in tiles_c0:
                cols, full = slice(j, j + w), slice(j, j + LANES)
                ct = pl.ds(pl.multiple_of(img * 16, 16), 16)
                cells = ev[ct, full] * cvec[0:1, full] * pmv[ct, :]
                up[j // LANES, pl.ds(0, 16, stride=2), :] = cells
                up[j // LANES, pl.ds(1, 16, stride=2), :] = cells
                scale = cvec[2:3, cols]
                for half in range(2):
                    at = pl.ds(pl.multiple_of(img * 64 + half * 32, 32), 32)
                    wide_cells = up[j // LANES, half * 16 : half * 16 + 16, 0:w]
                    wide_cells = jnp.concatenate([wide_cells, wide_cells], axis=0)
                    sv[at, cols] = (wide_cells + av[at, cols].astype(F32) * scale).astype(BF16)
        return carry

    lax.fori_loop(0, tiles // 4, part_grad, 0)
    red5.middle()
    lax.fori_loop(tiles // 4, 7 * tiles // 12, part_grad, 0)
    red_c.step_d()
    lax.fori_loop(7 * tiles // 12, tiles, part_grad, 0)
    red_a.step_f()
    total = red5.finish()
    red_c.step_e()
    pool_outs = [pool_own]
    for step in range(1, rows):
        pool_copies[step - 1].wait()
        sender = lax.rem(r + rows - step, rows)
        dst = pool_hbm.at[:, pl.ds(pl.multiple_of(sender * 16, 16), 16)]
        pool_outs.append(pltpu.make_async_copy(cotv.at[pl.ds(sender * own, own)], dst, pool_sems.at[2, step]))
        pool_outs[-1].start()
    mean1, inv1 = cvec[4:5, 0:c0], cvec[5:6, 0:c0]
    scale1, scale3 = cvec[6:7, 0:c0], cvec[7:8, 0:c0]
    shift_grad1 = 0.5 * unpack_row(total, 0, c0)
    gain_grad1 = inv1 * (0.5 * unpack_row(total, span, c0) - mean1 * shift_grad1)
    total = red6.finish()
    shift_grad3 = unpack_row(total, 0, c0)
    gain_grad3 = inv1 * (0.25 * unpack_row(total, span, c0) - mean1 * shift_grad3)
    slope1 = (scale3 * gain_grad3 + scale1 * gain_grad1) * inv1 * per
    const1 = (scale3 * shift_grad3 + scale1 * shift_grad1) * per - slope1 * mean1
    stats[...] = jnp.zeros_like(stats)
    stats[0:1, 0:c0] = gain_grad1
    stats[1:2, 0:c0] = shift_grad1
    stats[2:3, 0:bot] = gain_grad2
    stats[3:4, 0:bot] = shift_grad2
    stats[4:5, 0:c0] = gain_grad3
    stats[5:6, 0:c0] = shift_grad3
    stats[6:7, 0:LANES] = gain_grad_g
    stats[7:8, 0:LANES] = shift_grad_g
    stats[8:9, :] = jnp.broadcast_to(count_all, (1, stats.shape[1]))
    cvec[1:2, 0:c0] = const1
    cvec[3:4, 0:c0] = slope1

    def out_copy(t):
        at = pl.ds(pl.multiple_of(t * tp, tp), tp)
        return pltpu.make_async_copy(av.at[at], ig_hbm.at[at], x_sems.at[t])

    def last_body(t, carry):
        for q in range(TILE_IMGS):
            img = t * TILE_IMGS + q
            for j, w in tiles_c0:
                cols = slice(j, j + w)
                slope, const = cvec[3:4, cols], cvec[1:2, cols]
                for i in range(0, 64, 32):
                    at = pl.ds(pl.multiple_of(img * 64 + i, 32), 32)
                    value = (xv[at, cols].astype(F32) * slope + const) * mv[at, 0:w]
                    av[at, cols] = (sv[at, cols].astype(F32) - value).astype(BF16)
        out_copy(t).start()
        return carry

    lax.fori_loop(0, tiles // 2, last_body, 0)
    red_c.step_f()
    lax.fori_loop(tiles // 2, tiles, last_body, 0)
    red_a.finish()
    out_a = pltpu.make_async_copy(big[0][5], sum_a, io_sems.at[0])
    out_a.start()
    red_c.finish()
    out_c = pltpu.make_async_copy(big[1][5], sum_c, io_sems.at[2])
    out_c.start()
    for copy in pool_outs:
        copy.wait()
    for t in range(tiles):
        out_copy(t).wait()
    out_a.wait()
    out_c.wait()


def mm3(a, b, ca, cb):
    left = jnp.concatenate([a[0], a[0], a[1]], axis=ca)
    right = jnp.concatenate([b[0], b[1], b[0]], axis=cb)
    return dot(left, right, ca, cb)


def orthogonal_steps(pads, sides, sizes, found):
    start, gram, prod, ones = [], [], [], []
    for pad, side, size in zip(pads, sides, sizes):
        halves = unit_norm(pad)
        start.append(halves)
        gram.append(mm3(halves, halves, side, side))
        full = gram[-1].shape[0]
        i, j = (lax.broadcasted_iota(jnp.int32, (full, full), d) for d in (0, 1))
        ones.append((i == j) & (i < size))
        prod.append(None)
    yield
    for k in range(NS_STEPS):
        halves = [split(g) for g in gram]
        square = [mm3(h, h, 1, 0) for h in halves]
        poly = [jnp.where(o, QUINTIC_A, 0.0) + QUINTIC_B * g + QUINTIC_C * s for o, g, s in zip(ones, gram, square)]
        poly_h = [split(p) for p in poly]
        if k < NS_STEPS - 1:
            mid = [split(mm3(h, p, 1, 0)) for h, p in zip(halves, poly_h)]
            gram = [mm3(m, p, 1, 0) for m, p in zip(mid, poly_h)]
        prod = [p if k == 0 else split(mm3(q, p, 1, 0)) for q, p in zip(prod, poly_h)]
        if k == NS_STEPS - 1:
            found.extend(zip(start, prod))
        yield


def unit_norm(pad):
    value = pad[...]
    norm = jnp.sqrt(jnp.sum(jnp.sum(value * value, axis=0, keepdims=True), axis=1, keepdims=True)) + TINY
    pad[...] = value / norm
    return split(pad[...])


class LoopedOrthogonal:
    def __init__(self, valid, refs):
        self.valid = valid
        self.stack, self.poly, self.mid = refs
        self.full = self.poly.shape[1]

    @staticmethod
    def scratch(full):
        return [pltpu.VMEM((2, 2 * full, full), BF16), pltpu.VMEM((2, full, full), BF16), pltpu.VMEM((2, full, full), BF16)]

    def store(self, ref, start, value):
        high, low = split(value)
        ref[0, start : start + value.shape[0]] = high
        ref[1, start : start + value.shape[0]] = low

    def unit(self, scale):
        i, j = (lax.broadcasted_iota(jnp.int32, (self.full, self.full), d) for d in (0, 1))
        return jnp.where((i == j) & self.valid(i), scale, 0.0)

    def begin(self, gram):
        self.store(self.stack, 0, gram)
        self.stack[0, self.full :] = self.unit(1.0).astype(BF16)
        self.stack[1, self.full :] = jnp.zeros((self.full, self.full), BF16)

    def polynomial(self):
        n = self.full
        high, low = self.stack[0, 0:n], self.stack[1, 0:n]
        square = mm3((high, low), (high, low), 1, 0)
        gram = high.astype(F32) + low.astype(F32)
        self.store(self.poly, 0, self.unit(QUINTIC_A) + QUINTIC_B * gram + QUINTIC_C * square)

    def step(self, k, carry):
        n = self.full
        self.polynomial()
        poly = (self.poly[0], self.poly[1])
        both = mm3((self.stack[0], self.stack[1]), poly, 1, 0)
        self.store(self.mid, 0, both[0:n])
        self.store(self.stack, n, both[n:])
        self.store(self.stack, 0, mm3((self.mid[0], self.mid[1]), poly, 1, 0))
        return carry

    def light_step(self, k, carry):
        n = self.full
        high = self.stack[0, 0:n]
        gram = high.astype(F32) + self.stack[1, 0:n].astype(F32)
        poly = (QUINTIC_B * gram + QUINTIC_C * dot(high, high, 1, 0)).astype(BF16)
        self.poly[0] = poly
        both = self.stack[0].astype(F32) + self.stack[1].astype(F32)
        both = QUINTIC_A * both + dot(self.stack[0], poly, 1, 0)
        self.store(self.stack, n, both[n:])
        mid = both[0:n]
        self.store(self.stack, 0, QUINTIC_A * mid + dot(mid.astype(BF16), self.poly[0], 1, 0))
        return carry

    def finish(self):
        n = self.full
        self.polynomial()
        return split(mm3((self.stack[0, n:], self.stack[1, n:]), (self.poly[0], self.poly[1]), 1, 0))


def sum_rows(ref, top, count, width):
    base = top // 16 * 16
    size = min(round_up(top - base + count, 16), ref.shape[0] - base)
    return ref[base : base + size, :].astype(F32)[top - base : top - base + count, 0:width]


def transition_moment(c0, gr, trans, ml, sum_a, sum_c, base, put):
    stride_a, stride_g = round_up(c0, 16), round_up(gr, 8)
    for j, w in lane_tiles(trans):
        k = j // LANES
        put(slice(0, c0), slice(j, j + w), MOMENTUM_DECAY * ml[0:c0, j : j + w] + sum_rows(sum_a, k * stride_a, c0, w))
        rows = slice(c0, c0 + gr)
        put(rows, slice(j, j + w), MOMENTUM_DECAY * ml[rows, j : j + w] + sum_rows(sum_c, base + k * stride_g, gr, w))


def update_kernel(dims, ig_in, pool_in, wl_hbm, ml_hbm, stats, sum_a, sum_c, params, p_moment, wf, wg, mf, mg, *refs):
    (c0, bot, gr, trans) = dims
    cat = c0 + gr
    (ig_out, pool_out, wl_out, ml_out, p_moment_new, params_new, mf_new, mg_new, wf_new, wg_new) = refs[:10]
    (lpad, spad, igv, poolv, wl, ml, sems) = refs[10:17]
    low = round_up(bot, 8)
    loops = [
        LoopedOrthogonal(lambda i: i < trans, refs[17:20]),
        LoopedOrthogonal(lambda i: (i < bot) | ((i >= low) & (i < low + gr)), refs[20:23]),
    ]
    loads = [pltpu.make_async_copy(ml_hbm, ml, sems.at[0, 0]), pltpu.make_async_copy(wl_hbm, wl, sems.at[0, 1])]
    loads += [pltpu.make_async_copy(ig_in, igv, sems.at[0, 2]), pltpu.make_async_copy(pool_in, poolv, sems.at[0, 3])]
    stores = [pltpu.make_async_copy(ml, ml_out, sems.at[1, 0]), pltpu.make_async_copy(wl, wl_out, sems.at[1, 1])]
    stores += [pltpu.make_async_copy(igv, ig_out, sems.at[1, 2]), pltpu.make_async_copy(poolv, pool_out, sems.at[1, 3])]
    for copy in loads:
        copy.start()

    count = stats[8:9, 0:1]
    step = NORM_RATE * lax.rsqrt(count)
    spans = ((0, c0, 0), (c0, bot, 2), (c0 + bot, c0, 4), (2 * c0 + bot, gr, 6))
    for start, width, row in spans:
        moment = MOMENTUM_DECAY * p_moment[:, start : start + width] + stats[row : row + 2, 0:width]
        p_moment_new[:, start : start + width] = moment
        params_new[:, start : start + width] = params[:, start : start + width] - step * moment

    stride_g, stride_f = round_up(gr, 8), round_up(bot, 8)
    lpad[...] = jnp.zeros_like(lpad)
    spad[...] = jnp.zeros_like(spad)
    base = len(lane_tiles(c0)) * stride_f
    for j, w in lane_tiles(c0):
        new = MOMENTUM_DECAY * mf[:, j : j + w] + sum_rows(sum_c, j // LANES * stride_f, bot, w)
        mf_new[:, j : j + w] = new
        spad[0:bot, j : j + w] = new
    loads[0].wait()

    def put(at, cols, value):
        ml[at, cols] = value
        lpad[at, cols] = value

    transition_moment(c0, gr, trans, ml, sum_a, sum_c, base, put)
    stores[0].start()
    base = base + len(lane_tiles(trans)) * stride_g
    for j, w in lane_tiles(9 * bot):
        new = MOMENTUM_DECAY * mg[:, j : j + w] + sum_rows(sum_c, base + j // LANES * stride_g, gr, w)
        mg_new[:, j : j + w] = new
        spad[low : low + gr, j : j + w] = new
    halves = unit_norm(lpad)
    loops[0].begin(mm3(halves, halves, 0, 0))
    norms = []
    for start, stop in ((0, low), (low, low + round_up(gr, 8))):
        value = spad[start:stop, :]
        total = jnp.sum(jnp.sum(value * value, axis=0, keepdims=True), axis=1, keepdims=True)
        norms.append(1.0 / (jnp.sqrt(total) + TINY))
    row = lax.broadcasted_iota(jnp.int32, (spad.shape[0], 1), 0)
    spad[...] = spad[...] * jnp.where(row < low, norms[0], norms[1])
    halves = split(spad[...])
    gram = mm3(halves, halves, 1, 1)
    i, j = (lax.broadcasted_iota(jnp.int32, gram.shape, d) for d in (0, 1))
    loops[1].begin(jnp.where((i < low) == (j < low), gram, 0.0))
    for k in (2, 3):
        loads[k].wait()
        stores[k].start()

    def light(k, carry):
        loops[0].light_step(k, carry)
        loops[1].step(k, carry)
        return carry

    def full(k, carry):
        for loop in loops:
            loop.step(k, carry)
        return carry

    lax.fori_loop(0, 2, light, 0)
    lax.fori_loop(2, 4, full, 0)
    prods = [loop.finish() for loop in loops]
    ortho = mm3(split(lpad[...]), prods[0], 1, 0)
    loads[1].wait()
    wl[...] = wl[...] - MUON_RATE * ortho[0:cat, 0:trans]
    stores[1].start()
    ortho = mm3(prods[1], split(spad[...]), 1, 0)
    wf_new[...] = wf[...] - MUON_RATE * ortho[0:bot, 0:c0]
    wg_new[...] = wg[...] - MUON_RATE * ortho[low : low + gr, 0 : 9 * bot]
    for copy in stores:
        copy.wait()


def per_device(counts, inputs, small_flags, norm_params, norm_moment, w_bottleneck, w_growth, w_transition,
               m_bottleneck, m_growth, m_transition, cotangent):
    rows, batch = counts
    images, band, width, c0 = inputs.shape
    bot, gr, trans = w_bottleneck.shape[1], w_growth.shape[1], w_transition.shape[1]
    own = cotangent.shape[0]
    cat = c0 + gr
    n_pix, n_cell = images * 64, images * 16
    assert rows == 4 and band == 4 and width == 16 and images % 16 == 0
    any_spec = pl.BlockSpec(memory_space=pl.ANY)
    vmem_spec = pl.BlockSpec(memory_space=pltpu.VMEM)
    smem_spec = pl.BlockSpec(memory_space=pltpu.SMEM)
    wide = round_up(c0, LANES)
    unit = 16 * 4 * batch
    blocks = -(-trans // LANES)
    rows_b = -(-c0 // LANES) * round_up(bot, 8)
    rows_c = (blocks + -(-9 * bot // LANES)) * round_up(gr, 8)
    length_a = round_up(blocks * round_up(c0, 16), unit)
    length_c = round_up(rows_b + rows_c, unit)
    dims = (rows, batch, images, c0, bot, gr, trans, own)
    v = pltpu.VMEM
    dma = pltpu.SemaphoreType.DMA

    def vector_scratch(height):
        return [v((rows, height, LANES), F32), v((batch, height, LANES), F32), dma((2, rows)), dma((2, batch))]

    scratch = [
        v((n_pix, c0), BF16), v((n_pix, c0), BF16), v((n_pix, c0), BF16),
        v((n_pix, LANES), F32), v((n_cell, LANES), F32),
        v((n_cell, c0), F32), v((n_cell, c0), BF16), v((n_cell, LANES), BF16),
        v((n_cell, wide), F32), v((n_cell, LANES), F32), v((images, 16, trans), BF16),
        v((images, 4, 16, bot), F32),
        v((images, 6, 16, bot), BF16), v((n_pix, bot), BF16), v((n_pix, LANES), F32),
        v((images, 6, 16, LANES), BF16), v((n_pix, bot), F32),
        v((cat, trans), F32), v((cat, trans), BF16), v((LANES, trans), BF16),
        v((bot, c0), F32), v((bot, c0), BF16), v((c0, bot), BF16), v((gr, 9 * bot), F32),
        v((4, 3 * LANES, bot), F32), v((3, bot, 3 * LANES), BF16), v((3 * LANES, bot), BF16),
        v((TILE_IMGS * 16, TILE_IMGS * 64), BF16), v((TILE_IMGS * 64, TILE_IMGS * 16), BF16),
        v((8, wide), F32), v((8, LANES), F32), v((n_cell, LANES), F32),
        dma((images // TILE_IMGS,)), dma((5,)), dma((2, rows)), dma((2, 2)), dma((2, 2)), dma((3, rows)),
    ]
    for height in (16, 8, 8, 8):
        scratch += vector_scratch(height)
    scratch += [dma((2, rows)), dma((2, batch))] + vector_scratch(16)
    for length in (length_a, length_c):
        scratch += BlockReduce.scratch(length, batch)
    scratch += [v((wide // LANES, 32, LANES), F32)]
    scratch += [v((images, 16, trans), BF16)]
    struct = jax.ShapeDtypeStruct
    input_grad, pooled, stats, sum_a, sum_c = pl.pallas_call(
        functools.partial(band_kernel, dims),
        out_shape=(
            struct((n_pix, c0), BF16),
            struct((own, 64, trans), BF16),
            struct((16, wide), F32),
            struct((length_a, LANES), BF16),
            struct((length_c, LANES), BF16),
        ),
        in_specs=[smem_spec, any_spec, any_spec, vmem_spec, any_spec, any_spec, any_spec],
        out_specs=[any_spec, any_spec, vmem_spec, any_spec, any_spec],
        scratch_shapes=scratch,
        compiler_params=pltpu.CompilerParams(collective_id=0, has_side_effects=True, vmem_limit_bytes=VMEM_BYTES),
        name="band",
    )(
        small_flags,
        inputs.reshape(n_pix, c0),
        cotangent.reshape(own, 64, trans),
        norm_params,
        w_bottleneck.T,
        w_growth.T,
        w_transition,
    )
    vectors = [struct(norm_params.shape, F32)] * 2
    weights = [struct((bot, c0), F32), struct((gr, 9 * bot), F32)]
    outs = pl.pallas_call(
        functools.partial(update_kernel, (c0, bot, gr, trans)),
        out_shape=[struct((n_pix, c0), BF16), struct((own, 64, trans), BF16)]
        + [struct((cat, trans), F32)] * 2
        + vectors
        + weights * 2,
        in_specs=[any_spec] * 4 + [vmem_spec] * 9,
        out_specs=[any_spec] * 4 + [vmem_spec] * 6,
        scratch_shapes=[
            v((round_up(cat, 128), 4 * LANES), F32),
            v((round_up(bot + gr + 16, 256), round_up(max(c0, 9 * bot), LANES)), F32),
            v((n_pix, c0), BF16),
            v((own, 64, trans), BF16),
            v((cat, trans), F32),
            v((cat, trans), F32),
            dma((2, 4)),
        ]
        + LoopedOrthogonal.scratch(4 * LANES)
        + LoopedOrthogonal.scratch(round_up(bot + gr + 16, 256)),
        compiler_params=pltpu.CompilerParams(vmem_limit_bytes=VMEM_BYTES),
        name="update",
    )(
        input_grad, pooled, w_transition, m_transition, stats, sum_a, sum_c, norm_params, norm_moment, w_bottleneck.T,
        w_growth.T, m_bottleneck.T, m_growth.T,
    )
    (ig, pooled, wl_new, ml_new, moment_new, params_new, mf_new, mg_new, wf_new, wg_new) = outs
    return (
        pooled.reshape(cotangent.shape),
        ig.reshape(inputs.shape),
        moment_new,
        params_new,
        mf_new.T,
        mg_new.T,
        ml_new,
        wf_new.T,
        wg_new.T,
        wl_new,
    )


def solution(mesh):
    counts = (mesh.shape["rows"], mesh.shape["batch"])
    whole = (P(),) * 8
    images = P(("batch", "rows"), None, None, None)
    bands = P("batch", "rows", None, None)
    return jax.shard_map(
        functools.partial(per_device, counts),
        mesh=mesh,
        in_specs=(bands, P("batch")) + whole + (images,),
        out_specs=(images, bands) + whole,
        check_vma=False,
    )
```

time: 738 us -> 126 us (0.17); the launches traced: 729 us -> 126 us
  blocking collectives: 244 us -> 0 us
  matrix products: 134 us -> 0 us
  Pallas kernels: 0 us -> 125 us
  waiting for transfers between devices: 121 us -> 0 us
  local copies, waits for them, and re-layouts: 101 us -> 0 us
  other arithmetic: 92.2 us -> 0 us
  starting transfers between devices: 19.1 us -> 0 us
  between operations: 18 us -> 0.83 us
    psum x6 -> x0, blocking collectives: 244 us -> none  [the longest x2 81 us: per_device(): lax.psum((local_sum, local_square), ('batch', 'rows'))]
    dot_general x54 -> x0, matrix products: 134 us -> none  [the longest x15 26.4 us: gram_of(): return jnp.dot(row_part.T, row_part, precision=PRECISE)]
    pallas_call x0 -> x2, Pallas kernels: none -> 125 us  [the longest x1 96.6 us: per_device(): pl.pallas_call(functools.partial(band_kernel, dims), out_shape=(struct((n...]
    psum x1 -> x0, waiting for transfers between devices: 121 us -> none  [per_device(): lax.psum((grad_w_first, grad_w_taps, grad_w_last), ('batch', 'rows'))]
    reshape x3 -> x0, local copies, waits for them, and re-layouts: 38.3 us -> none  [the longest x1 28.9 us: forward_taps(): jnp.stack(pieces, axis=-1)]
    another operation x3 -> x0, local copies, waits for them, and re-layouts: 32.8 us -> none  [the longest x2 32.5 us: forward_taps(): jnp.stack(pieces, axis=-1)]
    reduce_sum x7 -> x0, other arithmetic: 22.7 us -> none  [the longest x1 9.24 us: per_device(): pooled = (0.25 * jnp.sum(grouped, axis=(2, 4))).astype(jnp.bfloat16)]
    convert_element_type x5 -> x0, other arithmetic: 21.5 us -> none  [the longest x1 14.2 us: per_device(): input_grad = (grad_joined[..., :in_chans] + first_back).astype(jnp.bfloat16)]
  transfers between devices with their start and end apart: 7 -> 0, of which waited for: 1 -> 0; matrix products, arithmetic and copies ran while one was open for 24% -> 0% of each run, Pallas kernels for 0% -> 0%
where the time goes in v1:
time: 126 us
  Pallas kernels  125 us (99%)
    pallas_call x1, Pallas kernels, per_device(): pl.pallas_call(functools.partial(band_kernel, dims), out_shape=(struct((n...  96.6 us
    pallas_call x1, Pallas kernels, per_device(): pl.pallas_call(functools.partial(update_kernel, (c0, bot, gr, trans)), ou...  28.4 us

profile of v1, /device:TPU:0, one launch (start us, length us, event | category | flops | bytes accessed | tf_op | source)
XLA Modules:
  0.0 125.8 jit_solution(854797528031159220)
XLA Ops:
  0.6 96.6 %band.1 = (bf16[3072,891]{1,0:T(8,128)(2,1)}, bf16[12,64,462]{2,1,0:T(8,128)(2,1)}, f32[16,896]{1,0:T(8,128)}, bf16[3584,128]{1,0:T(8,128)(2,1)}, bf16[1536,128]{1,0:T(8,128)(2,1)}) custom-call(s32[48]{0:T(128)} %flags.1, bf16[3072,891]{1,0:T(8,128)(2,1)} %bitcast.12, bf16[12,64,462]{2,1,0:T(8,128)(2,1)} %bitcast.17, f32[2,1947]{1,0:T(2,128)} %params.3, ...), custom_call_target="tpu_custom_call" | custom-call | tf_op jit(solution)/shard_map/band/pallas_call | solution.py:1108
  97.3 28.4 %update.1 = (bf16[3072,891]{1,0:T(8,128)(2,1)}, bf16[12,64,462]{2,1,0:T(8,128)(2,1)}, f32[924,462]{1,0:T(8,128)}, f32[924,462]{1,0:T(8,128)}, f32[2,1947]{1,0:T(...) custom-call(bf16[3072,891]{1,0:T(8,128)(2,1)} %get-tuple-element.25., ...), custom_call_target="tpu_custom_call" | custom-call | tf_op jit(solution)/shard_map/update/pallas_call | solution.py:1133

commit v2 on v1

--- a/solution.py
+++ b/solution.py
@@ -21,7 +21,7 @@
 BF16 = jnp.bfloat16
 MESH = pl.DeviceIdType.MESH
 LANES = 128
-TILE_IMGS = 4
+TILE_IMGS = 8
 VMEM_BYTES = 62 * 1024 * 1024
 
 
@@ -644,7 +644,7 @@
         pool_copies.append(
             pltpu.make_async_remote_copy(
                 src_ref=hpool.at[pl.ds(peer * own, own)],
-                dst_ref=cotv.at[pl.ds(r * own, own)],
+                dst_ref=pool_hbm.at[:, pl.ds(pl.multiple_of(r * 16, 16), 16)],
                 send_sem=pool_sems.at[0, step],
                 recv_sem=pool_sems.at[1, step],
                 device_id={"rows": peer},
@@ -693,12 +693,6 @@
     pack_row(slot, r, 2, row_sum(acc2))
     red4.start()
     red4.middle()
-    for copy in pool_copies:
-        copy.start()
-    pool_own = pltpu.make_async_copy(
-        hpool.at[pl.ds(r * own, own)], pool_hbm.at[:, pl.ds(pl.multiple_of(r * 16, 16), 16)], io_sems.at[4]
-    )
-    pool_own.start()
     red_a.step_e()
     gap = lax.broadcasted_iota(jnp.int32, (bot, 9 * bot), 1) - 9 * lax.broadcasted_iota(jnp.int32, (bot, 9 * bot), 0)
     value = jnp.zeros((gr, 9 * bot), F32)
@@ -718,6 +712,12 @@
     scale2 = gain2 * inv2
     slope2 = scale2 * gain_grad2 * inv2 * per
     const2 = scale2 * shift_grad2 * per - slope2 * mean2
+    for copy in pool_copies:
+        copy.start()
+    pool_own = pltpu.make_async_copy(
+        hpool.at[pl.ds(r * own, own)], pool_hbm.at[:, pl.ds(pl.multiple_of(r * 16, 16), 16)], io_sems.at[4]
+    )
+    pool_own.start()
 
     stride_f = round_up(bot, 8)
     blocks = -(-c0 // LANES)
@@ -793,13 +793,6 @@
     red_a.step_f()
     total = red5.finish()
     red_c.step_e()
-    pool_outs = [pool_own]
-    for step in range(1, rows):
-        pool_copies[step - 1].wait()
-        sender = lax.rem(r + rows - step, rows)
-        dst = pool_hbm.at[:, pl.ds(pl.multiple_of(sender * 16, 16), 16)]
-        pool_outs.append(pltpu.make_async_copy(cotv.at[pl.ds(sender * own, own)], dst, pool_sems.at[2, step]))
-        pool_outs[-1].start()
     mean1, inv1 = cvec[4:5, 0:c0], cvec[5:6, 0:c0]
     scale1, scale3 = cvec[6:7, 0:c0], cvec[7:8, 0:c0]
     shift_grad1 = 0.5 * unpack_row(total, 0, c0)
@@ -848,7 +841,8 @@
     red_c.finish()
     out_c = pltpu.make_async_copy(big[1][5], sum_c, io_sems.at[2])
     out_c.start()
-    for copy in pool_outs:
+    pool_own.wait()
+    for copy in pool_copies:
         copy.wait()
     for t in range(tiles):
         out_copy(t).wait()
@@ -1095,7 +1089,7 @@
         v((4, 3 * LANES, bot), F32), v((3, bot, 3 * LANES), BF16), v((3 * LANES, bot), BF16),
         v((TILE_IMGS * 16, TILE_IMGS * 64), BF16), v((TILE_IMGS * 64, TILE_IMGS * 16), BF16),
         v((8, wide), F32), v((8, LANES), F32), v((n_cell, LANES), F32),
-        dma((images // TILE_IMGS,)), dma((5,)), dma((2, rows)), dma((2, 2)), dma((2, 2)), dma((3, rows)),
+        dma((images // TILE_IMGS,)), dma((5,)), dma((2, rows)), dma((2, 2)), dma((2, 2)), dma((2, rows)),
     ]
     for height in (16, 8, 8, 8):
         scratch += vector_scratch(height)

time: 126 us -> 122 us (0.968)
  Pallas kernels: 125 us -> 121 us
    pallas_call x1, Pallas kernels: 96.6 us -> 92.6 us  [per_device(): pl.pallas_call(functools.partial(band_kernel, dims), out_shape=(struct((n...]
where the time goes in v2:
time: 122 us
  Pallas kernels  121 us (99%)
    pallas_call x1, Pallas kernels, per_device(): pl.pallas_call(functools.partial(band_kernel, dims), out_shape=(struct((n...  92.6 us
    pallas_call x1, Pallas kernels, per_device(): pl.pallas_call(functools.partial(update_kernel, (c0, bot, gr, trans)), ou...  28.4 us

profile of v2, /device:TPU:0, one launch (start us, length us, event | category | flops | bytes accessed | tf_op | source)
XLA Modules:
  0.0 121.8 jit_solution(6917438114158566910)
XLA Ops:
  0.6 92.6 %band.1 = (bf16[3072,891]{1,0:T(8,128)(2,1)}, bf16[12,64,462]{2,1,0:T(8,128)(2,1)}, f32[16,896]{1,0:T(8,128)}, bf16[3584,128]{1,0:T(8,128)(2,1)}, bf16[1536,128]{1,0:T(8,128)(2,1)}) custom-call(s32[48]{0:T(128)} %flags.1, bf16[3072,891]{1,0:T(8,128)(2,1)} %bitcast.12, bf16[12,64,462]{2,1,0:T(8,128)(2,1)} %bitcast.17, f32[2,1947]{1,0:T(2,128)} %params.3, ...), custom_call_target="tpu_custom_call" | custom-call | tf_op jit(solution)/shard_map/band/pallas_call | solution.py:1102
  93.2 28.4 %update.1 = (bf16[3072,891]{1,0:T(8,128)(2,1)}, bf16[12,64,462]{2,1,0:T(8,128)(2,1)}, f32[924,462]{1,0:T(8,128)}, f32[924,462]{1,0:T(8,128)}, f32[2,1947]{1,0:T(...) custom-call(bf16[3072,891]{1,0:T(8,128)(2,1)} %get-tuple-element.25., ...), custom_call_target="tpu_custom_call" | custom-call | tf_op jit(solution)/shard_map/update/pallas_call | solution.py:1127

commit v3 on v2

--- a/solution.py
+++ b/solution.py
@@ -505,7 +505,7 @@
     red_a = BlockReduce(place, counts, big[0])
     local_a = big[0][0]
     stride_a = round_up(c0, 16)
-    step_rows = 256
+    step_rows = 512
     for i in range(0, c0, step_rows):
         n = min(step_rows, c0 - i)
         value = dot(tin[:, i : i + n], cot_all, 0, 0)
@@ -582,12 +582,7 @@
         slot[r, j : j + 1, :] = row_sum(sums[j])
     red3.start()
 
-    def part_body(t, carry):
-        ct = pl.ds(pl.multiple_of(t * 256, 256), 256)
-        px[ct, 0:trans] = dot(tin[ct, :], wlb[0:c0, :], 1, 0)
-        return carry
-
-    lax.fori_loop(0, n_cell // 256, part_body, 0)
+    px[:, 0:trans] = dot(tin[...], wlb[0:c0, :], 1, 0)
     red3.middle()
     red_a.step_c()
     poolv[...] = jnp.zeros_like(poolv)

time: 122 us -> 122 us (level)
  no operation moved by 1% of the time
where the time goes in v3:
time: 122 us
  Pallas kernels  121 us (99%)
    pallas_call x1, Pallas kernels, per_device(): pl.pallas_call(functools.partial(band_kernel, dims), out_shape=(struct((n...  92.5 us
    pallas_call x1, Pallas kernels, per_device(): pl.pallas_call(functools.partial(update_kernel, (c0, bot, gr, trans)), ou...  28.4 us

profile of v3, /device:TPU:0, one launch (start us, length us, event | category | flops | bytes accessed | tf_op | source)
XLA Modules:
  0.0 121.7 jit_solution(6773609324218253735)
XLA Ops:
  0.6 92.5 %band.1 = (bf16[3072,891]{1,0:T(8,128)(2,1)}, bf16[12,64,462]{2,1,0:T(8,128)(2,1)}, f32[16,896]{1,0:T(8,128)}, bf16[3584,128]{1,0:T(8,128)(2,1)}, bf16[1536,128]{1,0:T(8,128)(2,1)}) custom-call(s32[48]{0:T(128)} %flags.1, bf16[3072,891]{1,0:T(8,128)(2,1)} %bitcast.12, bf16[12,64,462]{2,1,0:T(8,128)(2,1)} %bitcast.17, f32[2,1947]{1,0:T(2,128)} %params.3, ...), custom_call_target="tpu_custom_call" | custom-call | tf_op jit(solution)/shard_map/band/pallas_call | solution.py:1097
  93.1 28.4 %update.1 = (bf16[3072,891]{1,0:T(8,128)(2,1)}, bf16[12,64,462]{2,1,0:T(8,128)(2,1)}, f32[924,462]{1,0:T(8,128)}, f32[924,462]{1,0:T(8,128)}, f32[2,1947]{1,0:T(...) custom-call(bf16[3072,891]{1,0:T(8,128)(2,1)} %get-tuple-element.25., ...), custom_call_target="tpu_custom_call" | custom-call | tf_op jit(solution)/shard_map/update/pallas_call | solution.py:1122
